TPU v7x, 256 devices: a whole 4x4x8 slice. The times are simulated.
256 devices in a mesh: gx: 16 (over x, y), gy: 8 (over z), gz: 2 (over core).
Axes of the slice: x: 4, y: 4, z: 8, core: 2. Of those that a mesh axis runs over, the one named last changes fastest.
Arguments:
- fraction: float32 [32, 512, 1024], P('gz', 'gx', 'gy'), may hold values from 0 to 1
- velocity: float32 [3, 32, 512, 1024], P(None, 'gz', 'gx', 'gy'), may hold values from -0.45 to 0.45
- centres: int32 [3, 32768], P(None, ('gx', 'gy', 'gz')), may hold values from 3 to 130, as said below
- points: int32 [32768, 128], P(('gx', 'gy', 'gz')), may hold values from 0 to 342, as said below
- active_points: int32 [32768, 128], P(('gx', 'gy', 'gz')), may hold values 0 or 1
- counts: int32 [256], P(('gx', 'gy', 'gz')), may hold values from 1 to 128, as said below
- rigid_velocity_start: float32 [6, 32768], P(None, ('gx', 'gy', 'gz')), may hold values from -1.5 to 1.5
- inverse_mass: float32 [32768], P(('gx', 'gy', 'gz')), may hold values from 0.004 to 0.012
- inverse_inertia: float32 [32768], P(('gx', 'gy', 'gz')), may hold values from 0.01 to 0.03
Outputs:
- fraction_out: float32 [32, 512, 1024], P('gz', 'gx', 'gy')
- curvature: float32 [512, 1024], P('gx', 'gy')
- multipliers: float32 [3, 32768, 128], P(None, ('gx', 'gy', 'gz'))
- rigid_motion: float32 [6, 32768], P(None, ('gx', 'gy', 'gz'))
Inputs may be any that keep to these rules, and one draw needn't show every extreme that they name: `centres`: each component lies inside the slot's own brick in the widened block: 3 to 18 vertically, to 34 streamwise, to 130 spanwise. `points`: each code names a displacement of at most 3 cells along each direction. `counts`: bricks with even numbers (lower vertical half) own 128 // 2 to 128 particles, those with odd numbers 1 to 64.
All inputs are finite; a program needn't handle non-finite values. No bound on the sum of `active_points` on one device may be relied on, other than what follows from the above.
Results may differ from a plain program's by a relative error of at most 0.00014.
Values sent between devices are 32-bit elements; how exact they have to be, the bound alone decides.
A program may use at most 192 MiB of HBM per device.

v0:
```python
import jax
import jax.numpy as jnp
from jax import lax
from jax.sharding import PartitionSpec as P

POINT_REACH = 3
UZAWA = 2


RHO_STEP = 1.0
BETA_FLUID = 0.5


def extended(array, sides, width):
    for axis, dim in sides:
        size, length = (lax.axis_size(axis), array.shape[dim])
        up = [(i, (i + 1) % size) for i in range(size - 1)]
        down = [(j, i) for i, j in up]
        last = lax.slice_in_dim(array, length - width, length, axis=dim)
        first = lax.slice_in_dim(array, 0, width, axis=dim)
        before = lax.ppermute(last, axis, up)
        after = lax.ppermute(first, axis, down)
        array = jnp.concatenate([before, array, after], axis=dim)
    return array


def sweep_front(frac_pad, speed_pad):
    face_speed = 0.5 * (speed_pad[:-1] + speed_pad[1:])
    face_flux = (
        jnp.maximum(face_speed, 0.0) * frac_pad[:-1] + jnp.minimum(face_speed, 0.0) * frac_pad[1:]
    )
    interior = frac_pad[1:-1]
    return (
        interior - (face_flux[1:] - face_flux[:-1]) + interior * (face_speed[1:] - face_speed[:-1])
    )


def sweep_along(frac_pad, speed_pad, along_axis):
    result = sweep_front(
        jnp.moveaxis(frac_pad, along_axis, 0), jnp.moveaxis(speed_pad, along_axis, 0)
    )
    return jnp.moveaxis(result, 0, along_axis)


def curvature_of(height_pad):
    middle = height_pad[1:-1, 1:-1]
    east_side = height_pad[2:, 1:-1]
    west_side = height_pad[:-2, 1:-1]
    north_side = height_pad[1:-1, 2:]
    south_side = height_pad[1:-1, :-2]
    slope_x = 0.5 * (east_side - west_side)
    slope_y = 0.5 * (north_side - south_side)
    bend_xx = east_side - 2.0 * middle + west_side
    bend_yy = north_side - 2.0 * middle + south_side
    bend_xy = 0.25 * (
        height_pad[2:, 2:] - height_pad[2:, :-2] - height_pad[:-2, 2:] + height_pad[:-2, :-2]
    )
    metric = 1.0 + slope_x * slope_x + slope_y * slope_y
    top_part = (
        bend_xx * (1.0 + slope_y * slope_y)
        + bend_yy * (1.0 + slope_x * slope_x)
        - 2.0 * slope_x * slope_y * bend_xy
    )
    return top_part / (metric * jnp.sqrt(metric))


def cross_of(former, latter):
    return jnp.stack(
        [
            former[1] * latter[2] - former[2] * latter[1],
            former[2] * latter[0] - former[0] * latter[2],
            former[0] * latter[1] - former[1] * latter[0],
        ]
    )


def uzawa_steps(
    sampled, offsets, weight, rigid_velocity_start, inverse_mass, inverse_inertia, alive_mask
):
    multipliers = jnp.zeros_like(sampled)
    linear_start = rigid_velocity_start[:3]
    angular_start = rigid_velocity_start[3:]
    linear = linear_start
    angular = angular_start
    for iteration in range(UZAWA):
        moving = linear[:, :, None] + cross_of(angular[:, :, None], offsets)
        multipliers = (
            multipliers + RHO_STEP * (sampled - BETA_FLUID * multipliers - moving)
        ) * weight[None]
        net_force = jnp.sum(multipliers, axis=2)
        torque = jnp.sum(cross_of(offsets, multipliers), axis=2)
        linear = linear_start + inverse_mass[None] * net_force
        angular = angular_start + inverse_inertia[None] * torque
    rigid_motion = jnp.concatenate([linear, angular], axis=0) * alive_mask[None]
    return (multipliers, rigid_motion)


def probe_points(speed_ext, centres, shift_depth, shift_row, shift_col):
    extent_row = speed_ext.shape[2]
    extent_col = speed_ext.shape[3]
    cell_depth = centres[0][:, None] + shift_depth
    cell_row = centres[1][:, None] + shift_row
    cell_col = centres[2][:, None] + shift_col
    flat_index = (cell_depth * extent_row + cell_row) * extent_col + cell_col
    flat_speed = speed_ext.reshape(3, -1)
    picked = jnp.take(flat_speed, flat_index.reshape(-1), axis=1)
    return picked.reshape(3, flat_index.shape[0], flat_index.shape[1])


def body(
    fraction,
    velocity,
    centres,
    points,
    active_points,
    counts,
    rigid_velocity_start,
    inverse_mass,
    inverse_inertia,
):
    speed_ext = extended(velocity, (("gx", 2), ("gy", 3), ("gz", 1)), POINT_REACH)
    broadened_field = extended(jnp.stack([fraction, velocity[1]]), (("gx", 2),), 1)
    current = sweep_along(broadened_field[0], broadened_field[1], 1)
    broadened_field = extended(jnp.stack([current, velocity[2]]), (("gy", 3),), 1)
    current = sweep_along(broadened_field[0], broadened_field[1], 2)
    broadened_field = extended(jnp.stack([current, velocity[0]]), (("gz", 1),), 1)
    current = sweep_along(broadened_field[0], broadened_field[1], 0)
    partial_value = jnp.sum(current, axis=0)[None]
    layers = extended(partial_value, (("gx", 1), ("gy", 2), ("gz", 0)), 1)
    curvature = curvature_of(layers[0] + layers[1] + layers[2])
    shift_span = 2 * POINT_REACH + 1
    slot_count = points.shape[0]
    shift_depth = points // (shift_span * shift_span) - POINT_REACH
    shift_row = points // shift_span % shift_span - POINT_REACH
    shift_col = points % shift_span - POINT_REACH
    sampled = probe_points(speed_ext, centres, shift_depth, shift_row, shift_col)
    offsets = jnp.stack([shift_depth, shift_row, shift_col]).astype(jnp.float32)
    alive_mask = (jnp.arange(slot_count, dtype=jnp.int32) < counts[0]).astype(jnp.float32)
    weight = active_points.astype(jnp.float32) * alive_mask[:, None]
    multipliers, rigid_motion = uzawa_steps(
        sampled, offsets, weight, rigid_velocity_start, inverse_mass, inverse_inertia, alive_mask
    )
    return (current, curvature, multipliers, rigid_motion)


def solution(mesh):
    placed = (
        P("gz", "gx", "gy"),
        P(None, "gz", "gx", "gy"),
        P(None, ("gx", "gy", "gz")),
        P(("gx", "gy", "gz"), None),
        P(("gx", "gy", "gz"), None),
        P(("gx", "gy", "gz")),
        P(None, ("gx", "gy", "gz")),
        P(("gx", "gy", "gz")),
        P(("gx", "gy", "gz")),
    )
    return jax.shard_map(
        body,
        mesh=mesh,
        in_specs=placed,
        out_specs=(
            P("gz", "gx", "gy"),
            P("gx", "gy"),
            P(None, ("gx", "gy", "gz"), None),
            P(None, ("gx", "gy", "gz")),
        ),
        check_vma=False,
    )
```

profile of v0, /device:TPU:57, one launch (start us, length us, event | category | flops | bytes accessed | tf_op | source)
XLA Modules:
  0.0 235.5 jit_solution(9872419793228515867)
XLA Ops:
  0.6 1.1 fusion.44
  1.7 0.6 copy.45
  2.3 2.8 %collective-permute-start.12 = (f32[3,16,3,128]{3,1,2,0:T(8,128)}, f32[3,16,3,128]{3,1,2,0:T(8,128)S(1)}, u32[]{:S(2)}, u32[]{:S(2)}) collective-permute-start(f32[3,16,3,128]{3,1,2,0:T(8,128)} %copy.45), channel_id=1, source_target_pairs={{0,16},{16,32},{32,48},{48,64},{64,80},{80,96},{96,112},{112,128},... | collective-permute-start | bytes 221192 | tf_op jit(solution)/shard_map/ppermute | solution.py:21
  5.1 0.6 copy.46
  5.7 2.5 %collective-permute-start.13 = (f32[3,16,3,128]{3,1,2,0:T(8,128)}, f32[3,16,3,128]{3,1,2,0:T(8,128)}, u32[]{:S(2)}, u32[]{:S(2)}) collective-permute-start(f32[3,16,3,128]{3,1,2,0:T(8,128)} %copy.46), channel_id=1, source_target_pairs={{16,0},{32,16},{48,32},{64,48},{80,64},{96,80},{112,96},{128,112},... | collective-permute-start | bytes 221192 | tf_op jit(solution)/shard_map/ppermute | solution.py:22
  8.3 1.2 fusion.45
  9.4 0.9 pad_maximum_fusion.18
  10.3 4.9 %collective-permute-start = (f32[2,16,1,128]{3,2,1,0:T(1,128)S(1)}, f32[2,16,1,128]{3,2,1,0:T(1,128)S(1)}, u32[]{:S(2)}, u32[]{:S(2)}) collective-permute-start(f32[2,16,1,128]{3,2,1,0:T(1,128)S(1)} %get-tuple-element.37), channel_id=1, source_target_pairs={{0,16},{16,32},{32,48},{48,64},{64,80},{80,96},{96,112},{112,128},... | collective-permute-start | bytes 49160 | tf_op jit(solution)/shard_map/ppermute | solution.py:21
  15.2 1.9 collective-permute-start.1
  17.1 0.8 slice_bitcast_fusion.12
  17.9 1.0 fusion.29
  18.9 1.0 compare_and_fusion
  20.1 0.6 broadcast_clamp_fusion
  20.7 0.8 slice_bitcast_fusion.8
  21.5 0.3 collective-permute-done.1
  21.8 1.0 pad_maximum_fusion.7
  23.1 0.2 slice_maximum_fusion
  23.4 3.5 %collective-permute-start.2 = (f32[2,16,32,1]{3,2,1,0:T(8,128)S(1)}, f32[2,16,32,1]{3,2,1,0:T(8,128)S(1)}, u32[]{:S(2)}, u32[]{:S(2)}) collective-permute-start(f32[2,16,32,1]{3,2,1,0:T(8,128)S(1)} %get-tuple-element.35), channel_id=1, source_target_pairs={{0,2},{2,4},{4,6},{6,8},{8,10},{10,12},{12,14},{1,3},{3,5},{5,7},{... | collective-permute-start | bytes 12296 | tf_op jit(solution)/shard_map/ppermute | solution.py:21
  26.9 1.9 collective-permute-start.3
  28.8 0.8 multiply_subtract_fusion.11
  30.3 5.7 %collective-permute-done.2 = f32[2,16,32,1]{3,2,1,0:T(8,128)S(1)} collective-permute-done((f32[2,16,32,1]{3,2,1,0:T(8,128)S(1)}, f32[2,16,32,1]{3,2,1,0:T(8,128)S(1)}, u32[]{:S(2)}, u32[]{:S(2)}) %collective-permute-start.2) | collective-permute-done | bytes 4128 | tf_op jit(solution)/shard_map/ppermute | solution.py:21
  36.0 3.6 %collective-permute-done.3 = f32[2,16,32,1]{3,2,1,0:T(8,128)S(1)} collective-permute-done((f32[2,16,32,1]{3,2,1,0:T(8,128)S(1)}, f32[2,16,32,1]{3,2,1,0:T(8,128)S(1)}, u32[]{:S(2)}, u32[]{:S(2)}) %collective-permute-start.3) | collective-permute-done | bytes 4128 | tf_op jit(solution)/shard_map/ppermute | solution.py:22
  39.6 0.5 pad_maximum_fusion.1
  40.2 0.3 fusion
  40.6 0.3 fusion.12
  40.9 1.3 collective-permute-start.4
  42.2 5.6 %collective-permute-start.5 = (f32[2,1,32,128]{3,2,1,0:T(8,128)S(1)}, f32[2,1,32,128]{3,2,1,0:T(8,128)S(1)}, u32[]{:S(2)}, u32[]{:S(2)}) collective-permute-start(f32[2,1,32,128]{3,2,1,0:T(8,128)S(1)} %get-tuple-element.34), channel_id=1, source_target_pairs={{1,0},{3,2},{5,4},{7,6},{9,8},{11,10},{13,12},{15,14},{17,16},{19,... | collective-permute-start | bytes 98312 | tf_op jit(solution)/shard_map/ppermute | solution.py:22
  47.8 0.8 collective-permute-done.5
  48.9 0.8 fusion.39
  49.6 5.2 %collective-permute-start.6 = (f32[1,1,128]{2,1,0:T(1,128)S(1)}, f32[1,1,128]{2,1,0:T(1,128)S(1)}, u32[]{:S(2)}, u32[]{:S(2)}) collective-permute-start(f32[1,1,128]{2,1,0:T(1,128)S(1)} %get-tuple-element.56), channel_id=1, source_target_pairs={{0,16},{16,32},{32,48},{48,64},{64,80},{80,96},{96,112},{112,128},... | collective-permute-start | bytes 1544 | tf_op jit(solution)/shard_map/ppermute | solution.py:21
  54.8 1.9 collective-permute-start.7
  56.9 2.2 copy.36
  59.0 2.2 collective-permute-done.7
  61.3 4.7 %collective-permute-start.8 = (f32[1,34,1]{2,1,0:T(8,128)S(1)}, f32[1,34,1]{2,1,0:T(8,128)S(1)}, u32[]{:S(2)}, u32[]{:S(2)}) collective-permute-start(f32[1,34,1]{2,1,0:T(8,128)S(1)} %get-tuple-element.54), channel_id=1, source_target_pairs={{0,2},{2,4},{4,6},{6,8},{8,10},{10,12},{12,14},{1,3},{3,5},{5,7},{... | collective-permute-start | bytes 416 | tf_op jit(solution)/shard_map/ppermute | solution.py:21
  66.1 1.9 collective-permute-start.9
  68.0 3.8 %collective-permute-done.9 = f32[1,34,1]{2,1,0:T(8,128)S(1)} collective-permute-done((f32[1,34,1]{2,1,0:T(8,128)S(1)}, f32[1,34,1]{2,1,0:T(8,128)S(1)}, u32[]{:S(2)}, u32[]{:S(2)}) %collective-permute-start.9) | collective-permute-done | bytes 168 | tf_op jit(solution)/shard_map/ppermute | solution.py:22
  71.8 1.4 pad_maximum_fusion.13
  73.2 1.3 collective-permute-start.10
  74.5 6.0 %collective-permute-start.11 = (f32[1,34,130]{2,1,0:T(8,128)}, f32[1,34,130]{2,1,0:T(8,128)}, u32[]{:S(2)}, u32[]{:S(2)}) collective-permute-start(f32[1,34,130]{2,1,0:T(8,128)} %pad_maximum_fusion.13), channel_id=1, source_target_pairs={{1,0},{3,2},{5,4},{7,6},{9,8},{11,10},{13,12},{15,14},{17,16},{19,... | collective-permute-start | bytes 53048 | tf_op jit(solution)/shard_map/ppermute | solution.py:22
  80.5 2.2 copy.35
  82.7 3.0 %copy.37 = f32[3,16,3,128]{2,1,3,0:T(8,128)} copy(f32[3,16,3,128]{3,1,2,0:T(8,128)} %collective-permute-done.13) | data formatting | bytes 147456 | tf_op jit(solution)/shard_map/ppermute | solution.py:22
  85.8 1.3 pad_maximum_fusion.12
  87.1 3.8 %collective-permute-start.14 = (f32[3,16,38,3]{2,1,3,0:T(8,128)S(1)}, f32[3,16,38,3]{2,1,3,0:T(8,128)S(1)}, u32[]{:S(2)}, u32[]{:S(2)}) collective-permute-start(f32[3,16,38,3]{2,1,3,0:T(8,128)S(1)} %get-tuple-element.20), channel_id=1, source_target_pairs={{0,2},{2,4},{4,6},{6,8},{8,10},{10,12},{12,14},{1,3},{3,5},{5,7},{... | collective-permute-start | bytes 65672 | tf_op jit(solution)/shard_map/ppermute | solution.py:21
  90.9 1.9 collective-permute-start.15
  92.8 0.9 add_bitcast_fusion
  93.7 2.6 %collective-permute-done.15 = f32[3,16,38,3]{2,1,3,0:T(8,128)S(1)} collective-permute-done((f32[3,16,38,3]{2,1,3,0:T(8,128)S(1)}, f32[3,16,38,3]{2,1,3,0:T(8,128)S(1)}, u32[]{:S(2)}, u32[]{:S(2)}) %collective-permute-start.15) | collective-permute-done | bytes 21920 | tf_op jit(solution)/shard_map/ppermute | solution.py:22
  96.3 2.9 %pad_maximum_fusion.6 = (f32[3,3,38,134]{2,1,3,0:T(4,128)}, f32[3,3,38,134]{2,1,3,0:T(4,128)}) fusion(f32[3,16,38,3]{2,1,3,0:T(8,128)S(1)} %collective-permute-done.15, f32[3,16,38,3]{2,1,3,0:T(8,128)S(1)} %collective-permute-done.14, f32[3,16,3,128]{2,1,3,0:T(8,128)S(1)} %copy-done.1, f32[3,16,32,128]{2,1,3,0:T(8,128)S(1)} %copy.36, ...), kind=kLoop, calls=%fused_computation.7 | loop fusion | flops 366624 | bytes 1344288 | tf_op jit(solution)/shard_map/slice | solution.py:19
  99.2 2.3 copy.38
  101.5 1.3 collective-permute-start.16
  102.7 2.3 copy.39
  105.0 4.5 %collective-permute-start.17 = (f32[3,3,38,134]{3,2,1,0:T(8,128)}, f32[3,3,38,134]{3,2,1,0:T(8,128)}, u32[]{:S(2)}, u32[]{:S(2)}) collective-permute-start(f32[3,3,38,134]{3,2,1,0:T(8,128)} %copy.39), channel_id=1, source_target_pairs={{1,0},{3,2},{5,4},{7,6},{9,8},{11,10},{13,12},{15,14},{17,16},{19,... | collective-permute-start | bytes 549944 | tf_op jit(solution)/shard_map/ppermute | solution.py:22
  109.6 0.7 fusion.30
  110.3 2.4 %copy.40 = f32[3,3,38,134]{2,1,3,0:T(4,128)} copy(f32[3,3,38,134]{3,2,1,0:T(8,128)} %collective-permute-done.16) | data formatting | bytes 366624 | tf_op jit(solution)/shard_map/ppermute | solution.py:21
  112.7 2.5 %copy.41 = f32[3,3,38,134]{2,1,3,0:T(4,128)} copy(f32[3,3,38,134]{3,2,1,0:T(8,128)} %collective-permute-done.17) | data formatting | bytes 366624 | tf_op jit(solution)/shard_map/ppermute | solution.py:22
  115.2 7.3 %pad_maximum_fusion = f32[3,22,38,134]{2,1,3,0:T(8,128)} fusion(f32[3,3,38,134]{2,1,3,0:T(4,128)} %copy.41, f32[3,16,38,3]{2,1,3,0:T(8,128)} %copy-done.3, f32[3,16,3,128]{2,1,3,0:T(8,128)} %copy.37, f32[3,16,32,128]{2,1,3,0:T(8,128)S(1)} %copy.36, f32[3,16,3,128]{2,1,3,0:T(8,128)} %copy.35, f32[3,16,38,3]{2,1,3,0:T(8,128)S(1)} %collective-permute-done.14, ...), kind=kLoop, calls=%fused_computation.1 | loop fusion | flops 2016432 | bytes 2688576 | tf_op jit(solution)/shard_map/concatenate | solution.py:23
  122.5 4.7 %copy.42 = f32[3,22,38,134]{3,2,1,0:T(8,128)S(1)} copy(f32[3,22,38,134]{2,1,3,0:T(8,128)} %pad_maximum_fusion) | data formatting | bytes 2688576 | tf_op jit(solution)/shard_map/concatenate | solution.py:23
  127.2 3.4 %reshape.182 = f32[3,112024]{1,0:T(4,128)} reshape(f32[3,22,38,134]{3,2,1,0:T(8,128)S(1)} %copy.42) | data formatting | bytes 2688576 | tf_op jit(solution)/shard_map/reshape | solution.py:105
  130.6 26.1 %copy.43 = f32[3,112024]{0,1:T(8,128)} copy(f32[3,112024]{1,0:T(4,128)} %reshape.182) | data formatting | bytes 2688576 | tf_op jit(solution)/shard_map/reshape | solution.py:105
  156.7 71.8 %gather_fusion = f32[16384,3]{1,0:T(8,128)} fusion(f32[3,112024]{0,1:T(8,128)} %copy.43, s32[16384]{0:T(1024)S(1)} %copy-done.4), kind=kCustom, calls=%fused_computation | custom fusion | bytes 458752 | tf_op jit(solution)/shard_map/jit(_take)/gather | solution.py:106
  228.5 5.3 %copy.44 = f32[3,128,128]{2,1,0:T(8,128)S(1)} copy(f32[3,128,128]{0,2,1:T(8,128)} %bitcast.74) | data formatting | bytes 393216 | tf_op jit(solution)/shard_map/jit(_take)/gather | solution.py:106
  233.8 0.2 fusion.37
  234.1 0.1 maximum_reduce_fusion
  234.4 0.2 fusion.35
  234.8 0.6 maximum_multiply_fusion
  (74 shorter events, 1.3 us)
Async XLA Ops:
  2.3 78.2 %collective-permute-start.12 = (f32[3,16,3,128]{3,1,2,0:T(8,128)}, f32[3,16,3,128]{3,1,2,0:T(8,128)S(1)}, u32[]{:S(2)}, u32[]{:S(2)}) collective-permute-start(f32[3,16,3,128]{3,1,2,0:T(8,128)} %copy.45), channel_id=1, source_target_pairs={{0,16},{16,32},{32,48},{48,64},{64,80},{80,96},{96,112},{112,128},... | collective-permute-start | bytes 221192 | tf_op jit(solution)/shard_map/ppermute | solution.py:21
  5.7 77.0 %collective-permute-start.13 = (f32[3,16,3,128]{3,1,2,0:T(8,128)}, f32[3,16,3,128]{3,1,2,0:T(8,128)}, u32[]{:S(2)}, u32[]{:S(2)}) collective-permute-start(f32[3,16,3,128]{3,1,2,0:T(8,128)} %copy.46), channel_id=1, source_target_pairs={{16,0},{32,16},{48,32},{64,48},{80,64},{96,80},{112,96},{128,112},... | collective-permute-start | bytes 221192 | tf_op jit(solution)/shard_map/ppermute | solution.py:22
  10.3 11.2 %collective-permute-start = (f32[2,16,1,128]{3,2,1,0:T(1,128)S(1)}, f32[2,16,1,128]{3,2,1,0:T(1,128)S(1)}, u32[]{:S(2)}, u32[]{:S(2)}) collective-permute-start(f32[2,16,1,128]{3,2,1,0:T(1,128)S(1)} %get-tuple-element.37), channel_id=1, source_target_pairs={{0,16},{16,32},{32,48},{48,64},{64,80},{80,96},{96,112},{112,128},... | collective-permute-start | bytes 49160 | tf_op jit(solution)/shard_map/ppermute | solution.py:21
  15.2 6.6 %collective-permute-start.1 = (f32[2,16,1,128]{3,2,1,0:T(1,128)S(1)}, f32[2,16,1,128]{3,2,1,0:T(1,128)S(1)}, u32[]{:S(2)}, u32[]{:S(2)}) collective-permute-start(f32[2,16,1,128]{3,2,1,0:T(1,128)S(1)} %get-tuple-element.38), channel_id=1, source_target_pairs={{16,0},{32,16},{48,32},{64,48},{80,64},{96,80},{112,96},{128,112},... | collective-permute-start | bytes 49160 | tf_op jit(solution)/shard_map/ppermute | solution.py:22
  23.4 12.6 %collective-permute-start.2 = (f32[2,16,32,1]{3,2,1,0:T(8,128)S(1)}, f32[2,16,32,1]{3,2,1,0:T(8,128)S(1)}, u32[]{:S(2)}, u32[]{:S(2)}) collective-permute-start(f32[2,16,32,1]{3,2,1,0:T(8,128)S(1)} %get-tuple-element.35), channel_id=1, source_target_pairs={{0,2},{2,4},{4,6},{6,8},{8,10},{10,12},{12,14},{1,3},{3,5},{5,7},{... | collective-permute-start | bytes 12296 | tf_op jit(solution)/shard_map/ppermute | solution.py:21
  26.9 12.7 %collective-permute-start.3 = (f32[2,16,32,1]{3,2,1,0:T(8,128)S(1)}, f32[2,16,32,1]{3,2,1,0:T(8,128)S(1)}, u32[]{:S(2)}, u32[]{:S(2)}) collective-permute-start(f32[2,16,32,1]{3,2,1,0:T(8,128)S(1)} %get-tuple-element.36), channel_id=1, source_target_pairs={{2,0},{4,2},{6,4},{8,6},{10,8},{12,10},{14,12},{3,1},{5,3},{7,5},{... | collective-permute-start | bytes 12296 | tf_op jit(solution)/shard_map/ppermute | solution.py:22
  40.2 16.5 %copy-start.10 = (s32[128,128]{1,0:T(8,128)S(1)}, s32[128,128]{1,0:T(8,128)}, u32[]{:S(2)}) copy-start(s32[128,128]{1,0:T(8,128)} %param.13) | copy-start | bytes 196612
  40.9 6.9 %collective-permute-start.4 = (f32[2,1,32,128]{3,2,1,0:T(8,128)S(1)}, f32[2,1,32,128]{3,2,1,0:T(8,128)S(1)}, u32[]{:S(2)}, u32[]{:S(2)}) collective-permute-start(f32[2,1,32,128]{3,2,1,0:T(8,128)S(1)} %get-tuple-element.33), channel_id=1, source_target_pairs={{0,1},{2,3},{4,5},{6,7},{8,9},{10,11},{12,13},{14,15},{16,17},{18,... | collective-permute-start | bytes 98312 | tf_op jit(solution)/shard_map/ppermute | solution.py:21
  42.2 6.4 %collective-permute-start.5 = (f32[2,1,32,128]{3,2,1,0:T(8,128)S(1)}, f32[2,1,32,128]{3,2,1,0:T(8,128)S(1)}, u32[]{:S(2)}, u32[]{:S(2)}) collective-permute-start(f32[2,1,32,128]{3,2,1,0:T(8,128)S(1)} %get-tuple-element.34), channel_id=1, source_target_pairs={{1,0},{3,2},{5,4},{7,6},{9,8},{11,10},{13,12},{15,14},{17,16},{19,... | collective-permute-start | bytes 98312 | tf_op jit(solution)/shard_map/ppermute | solution.py:22
  47.8 9.0 %copy-start.16 = (f32[128]{0:T(128)}, f32[128]{0:T(128)S(1)}, u32[]{:S(2)}) copy-start(f32[128]{0:T(128)S(1)} %compare_convert_fusion) | copy-start | bytes 1540
  49.6 9.4 %collective-permute-start.6 = (f32[1,1,128]{2,1,0:T(1,128)S(1)}, f32[1,1,128]{2,1,0:T(1,128)S(1)}, u32[]{:S(2)}, u32[]{:S(2)}) collective-permute-start(f32[1,1,128]{2,1,0:T(1,128)S(1)} %get-tuple-element.56), channel_id=1, source_target_pairs={{0,16},{16,32},{32,48},{48,64},{64,80},{80,96},{96,112},{112,128},... | collective-permute-start | bytes 1544 | tf_op jit(solution)/shard_map/ppermute | solution.py:21
  54.8 6.4 %collective-permute-start.7 = (f32[1,1,128]{2,1,0:T(1,128)S(1)}, f32[1,1,128]{2,1,0:T(1,128)S(1)}, u32[]{:S(2)}, u32[]{:S(2)}) collective-permute-start(f32[1,1,128]{2,1,0:T(1,128)S(1)} %get-tuple-element.57), channel_id=1, source_target_pairs={{16,0},{32,16},{48,32},{64,48},{80,64},{96,80},{112,96},{128,112},... | collective-permute-start | bytes 1544 | tf_op jit(solution)/shard_map/ppermute | solution.py:22
  59.0 7.0 %copy-start.12 = (f32[1,1,128]{2,1,0:T(1,128)}, f32[1,1,128]{2,1,0:T(1,128)S(1)}, u32[]{:S(2)}) copy-start(f32[1,1,128]{2,1,0:T(1,128)S(1)} %collective-permute-done.6) | copy-start | bytes 1540
  61.2 4.9 %copy-start.14 = (f32[1,1,128]{2,1,0:T(1,128)}, f32[1,1,128]{2,1,0:T(1,128)S(1)}, u32[]{:S(2)}) copy-start(f32[1,1,128]{2,1,0:T(1,128)S(1)} %collective-permute-done.7) | copy-start | bytes 1540
  61.3 6.7 %collective-permute-start.8 = (f32[1,34,1]{2,1,0:T(8,128)S(1)}, f32[1,34,1]{2,1,0:T(8,128)S(1)}, u32[]{:S(2)}, u32[]{:S(2)}) collective-permute-start(f32[1,34,1]{2,1,0:T(8,128)S(1)} %get-tuple-element.54), channel_id=1, source_target_pairs={{0,2},{2,4},{4,6},{6,8},{8,10},{10,12},{12,14},{1,3},{3,5},{5,7},{... | collective-permute-start | bytes 416 | tf_op jit(solution)/shard_map/ppermute | solution.py:21
  66.1 5.7 %collective-permute-start.9 = (f32[1,34,1]{2,1,0:T(8,128)S(1)}, f32[1,34,1]{2,1,0:T(8,128)S(1)}, u32[]{:S(2)}, u32[]{:S(2)}) collective-permute-start(f32[1,34,1]{2,1,0:T(8,128)S(1)} %get-tuple-element.55), channel_id=1, source_target_pairs={{2,0},{4,2},{6,4},{8,6},{10,8},{12,10},{14,12},{3,1},{5,3},{7,5},{... | collective-permute-start | bytes 416 | tf_op jit(solution)/shard_map/ppermute | solution.py:22
  68.0 19.0 %copy-start.8 = (f32[1,34,1]{2,1,0:T(8,128)}, f32[1,34,1]{2,1,0:T(8,128)S(1)}, u32[]{:S(2)}) copy-start(f32[1,34,1]{2,1,0:T(8,128)S(1)} %collective-permute-done.8) | copy-start | bytes 412
  71.8 15.3 %copy-start.9 = (f32[1,34,1]{2,1,0:T(8,128)}, f32[1,34,1]{2,1,0:T(8,128)S(1)}, u32[]{:S(2)}) copy-start(f32[1,34,1]{2,1,0:T(8,128)S(1)} %collective-permute-done.9) | copy-start | bytes 412
  73.2 19.6 %collective-permute-start.10 = (f32[1,34,130]{2,1,0:T(8,128)}, f32[1,34,130]{2,1,0:T(8,128)}, u32[]{:S(2)}, u32[]{:S(2)}) collective-permute-start(f32[1,34,130]{2,1,0:T(8,128)} %pad_maximum_fusion.13), channel_id=1, source_target_pairs={{0,1},{2,3},{4,5},{6,7},{8,9},{10,11},{12,13},{14,15},{16,17},{18,... | collective-permute-start | bytes 53048 | tf_op jit(solution)/shard_map/ppermute | solution.py:21
  74.5 18.3 %collective-permute-start.11 = (f32[1,34,130]{2,1,0:T(8,128)}, f32[1,34,130]{2,1,0:T(8,128)}, u32[]{:S(2)}, u32[]{:S(2)}) collective-permute-start(f32[1,34,130]{2,1,0:T(8,128)} %pad_maximum_fusion.13), channel_id=1, source_target_pairs={{1,0},{3,2},{5,4},{7,6},{9,8},{11,10},{13,12},{15,14},{17,16},{19,... | collective-permute-start | bytes 53048 | tf_op jit(solution)/shard_map/ppermute | solution.py:22
  85.8 7.1 %copy-start.13 = (f32[1,1,128]{2,1,0:T(1,128)S(1)}, f32[1,1,128]{2,1,0:T(1,128)}, u32[]{:S(2)}) copy-start(f32[1,1,128]{2,1,0:T(1,128)} %copy-done.12) | copy-start | bytes 1540
  85.8 7.1 %copy-start.15 = (f32[1,1,128]{2,1,0:T(1,128)S(1)}, f32[1,1,128]{2,1,0:T(1,128)}, u32[]{:S(2)}) copy-start(f32[1,1,128]{2,1,0:T(1,128)} %copy-done.14) | copy-start | bytes 1540
  85.8 10.5 %copy-start = (f32[3,16,3,128]{2,1,3,0:T(8,128)S(1)}, f32[3,16,3,128]{2,1,3,0:T(8,128)}, u32[]{:S(2)}) copy-start(f32[3,16,3,128]{2,1,3,0:T(8,128)} %copy.35) | copy-start | bytes 221188
  85.8 10.5 %copy-start.1 = (f32[3,16,3,128]{2,1,3,0:T(8,128)S(1)}, f32[3,16,3,128]{2,1,3,0:T(8,128)}, u32[]{:S(2)}) copy-start(f32[3,16,3,128]{2,1,3,0:T(8,128)} %copy.37) | copy-start | bytes 221188
  87.1 6.7 %collective-permute-start.14 = (f32[3,16,38,3]{2,1,3,0:T(8,128)S(1)}, f32[3,16,38,3]{2,1,3,0:T(8,128)S(1)}, u32[]{:S(2)}, u32[]{:S(2)}) collective-permute-start(f32[3,16,38,3]{2,1,3,0:T(8,128)S(1)} %get-tuple-element.20), channel_id=1, source_target_pairs={{0,2},{2,4},{4,6},{6,8},{8,10},{10,12},{12,14},{1,3},{3,5},{5,7},{... | collective-permute-start | bytes 65672 | tf_op jit(solution)/shard_map/ppermute | solution.py:21
  90.9 5.4 %collective-permute-start.15 = (f32[3,16,38,3]{2,1,3,0:T(8,128)S(1)}, f32[3,16,38,3]{2,1,3,0:T(8,128)S(1)}, u32[]{:S(2)}, u32[]{:S(2)}) collective-permute-start(f32[3,16,38,3]{2,1,3,0:T(8,128)S(1)} %get-tuple-element.21), channel_id=1, source_target_pairs={{2,0},{4,2},{6,4},{8,6},{10,8},{12,10},{14,12},{3,1},{5,3},{7,5},{... | collective-permute-start | bytes 65672 | tf_op jit(solution)/shard_map/ppermute | solution.py:22
  96.3 2.9 %copy-start.3 = (f32[3,16,38,3]{2,1,3,0:T(8,128)}, f32[3,16,38,3]{2,1,3,0:T(8,128)S(1)}, u32[]{:S(2)}) copy-start(f32[3,16,38,3]{2,1,3,0:T(8,128)S(1)} %collective-permute-done.15) | copy-start | bytes 65668
  101.5 8.8 %collective-permute-start.16 = (f32[3,3,38,134]{3,2,1,0:T(8,128)}, f32[3,3,38,134]{3,2,1,0:T(8,128)}, u32[]{:S(2)}, u32[]{:S(2)}) collective-permute-start(f32[3,3,38,134]{3,2,1,0:T(8,128)} %copy.38), channel_id=1, source_target_pairs={{0,1},{2,3},{4,5},{6,7},{8,9},{10,11},{12,13},{14,15},{16,17},{18,... | collective-permute-start | bytes 549944 | tf_op jit(solution)/shard_map/ppermute | solution.py:21
  105.0 7.7 %collective-permute-start.17 = (f32[3,3,38,134]{3,2,1,0:T(8,128)}, f32[3,3,38,134]{3,2,1,0:T(8,128)}, u32[]{:S(2)}, u32[]{:S(2)}) collective-permute-start(f32[3,3,38,134]{3,2,1,0:T(8,128)} %copy.39), channel_id=1, source_target_pairs={{1,0},{3,2},{5,4},{7,6},{9,8},{11,10},{13,12},{15,14},{17,16},{19,... | collective-permute-start | bytes 549944 | tf_op jit(solution)/shard_map/ppermute | solution.py:22
  130.5 26.1 %copy-start.4 = (s32[16384]{0:T(1024)S(1)}, s32[16384]{0:T(1024)}, u32[]{:S(2)}) copy-start(s32[16384]{0:T(1024)} %broadcast_clamp_fusion) | copy-start | bytes 196612
  156.6 77.1 %copy-start.5 = (f32[1,128,128]{2,1,0:T(8,128)S(1)}, f32[1,128,128]{2,1,0:T(8,128)}, u32[]{:S(2)}) copy-start(f32[1,128,128]{2,1,0:T(8,128)} %get-tuple-element.48) | copy-start | bytes 196612
  156.6 77.1 %copy-start.6 = (f32[1,128,128]{2,1,0:T(8,128)S(1)}, f32[1,128,128]{2,1,0:T(8,128)}, u32[]{:S(2)}) copy-start(f32[1,128,128]{2,1,0:T(8,128)} %get-tuple-element.49) | copy-start | bytes 196612
  156.6 77.1 %copy-start.7 = (f32[1,128,128]{2,1,0:T(8,128)S(1)}, f32[1,128,128]{2,1,0:T(8,128)}, u32[]{:S(2)}) copy-start(f32[1,128,128]{2,1,0:T(8,128)} %get-tuple-element.50) | copy-start | bytes 196612
  156.7 77.1 %slice-start = ((f32[6,128]{1,0:T(8,128)}), f32[3,128]{1,0:T(4,128)S(1)}, s32[]{:S(2)}) async-start(f32[6,128]{1,0:T(8,128)} %param.15), calls=%async_computation | async-start | bytes 4096 | tf_op jit(solution)/shard_map/slice | solution.py:81
  228.5 5.7 %copy-start.11 = (f32[6,128]{1,0:T(8,128)S(1)}, f32[6,128]{1,0:T(8,128)}, u32[]{:S(2)}) copy-start(f32[6,128]{1,0:T(8,128)} %param.15) | copy-start | bytes 9220
  228.5 5.7 %copy-start.18 = (f32[128]{0:T(128)S(1)}, f32[128]{0:T(128)}, u32[]{:S(2)}) copy-start(f32[128]{0:T(128)} %param.16) | copy-start | bytes 1540
  228.5 5.7 %copy-start.19 = (f32[128]{0:T(128)S(1)}, f32[128]{0:T(128)}, u32[]{:S(2)}) copy-start(f32[128]{0:T(128)} %param.17) | copy-start | bytes 1540
  228.5 6.3 %copy-start.17 = (f32[128]{0:T(128)S(1)}, f32[128]{0:T(128)}, u32[]{:S(2)}) copy-start(f32[128]{0:T(128)} %copy-done.16) | copy-start | bytes 1540
  234.6 0.8 copy-start.2
where the time goes:
time: 237 us; the launch traced here: 235 us
  local copies, waits for them, and re-layouts  133 us (56%)
  starting transfers between devices  57 us (24%)
  other arithmetic  24.1 us (10%)
  waiting for transfers between devices  19 us (8%)
    gather x2, local copies, waits for them, and re-layouts, probe_points(): picked = jnp.take(flat_speed, flat_index.reshape(-1), axis=1)  77.1 us
    reshape x2, local copies, waits for them, and re-layouts, probe_points(): flat_speed = speed_ext.reshape(3, -1)  29.5 us
    ppermute x9, starting transfers between devices, extended(): before = lax.ppermute(last, axis, up)  28.7 us
    ppermute x9, starting transfers between devices, extended(): after = lax.ppermute(first, axis, down)  28.3 us
    ppermute x9, waiting for transfers between devices, extended(): after = lax.ppermute(first, axis, down)  13.3 us
    concatenate x6, other arithmetic, extended(): array = jnp.concatenate([before, array, after], axis=dim)  10.4 us
    ppermute x9, waiting for transfers between devices, extended(): before = lax.ppermute(last, axis, up)  5.73 us
    ppermute x2, local copies, waits for them, and re-layouts, extended(): after = lax.ppermute(first, axis, down)  5.48 us
  transfers between devices with their start and end apart: 18, of which 7 were waited for; matrix products, arithmetic and copies ran while one was open for 12% of the time, Pallas kernels for 0%

commit v1 on v0

v1 whole, which is shorter than its diff:
```python
import jax
import jax.numpy as jnp
from jax import lax
from jax.experimental import pallas as pl
from jax.experimental.pallas import tpu as pltpu
from jax.sharding import PartitionSpec as P

MESH = pl.DeviceIdType.MESH
F32 = jnp.float32
I32 = jnp.int32

ACROSS = [(dx, dy) for dx in (-1, 0, 1) for dy in (-1, 0, 1) if dx or dy]


def lanes_of(shape):
    return lax.broadcasted_iota(I32, shape, len(shape) - 1)


def turn(x, by):
    by %= 128
    return pltpu.roll(x, by, x.ndim - 1) if by else x


def halo_kernel(
    frac, vel, T, fout, curv,
    F, QU, QD, RQL, RQH, PL, PR, RL, RR, RZ, RZF, SQ, HB, HP, HX, HY, HC, HS, HN, HM,
    in_sem, send, recv, hsend, hrecv,
):
    gx, gy, gz = (lax.axis_index(a) for a in ("gx", "gy", "gz"))

    def place(dx, dy, dz):
        return (lax.rem(gx + dx + 16, 16), lax.rem(gy + dy + 8, 8), gz if dz == 0 else 1 - gz)

    everyone = [(dx, dy, dz) for dz in (0, 1) for dx, dy in ACROSS] + [(0, 0, 1)]
    own = []
    for side in (0, 1):
        own.append(pltpu.make_async_copy(vel, T.at[side, :, 4:20, 8:40, :], in_sem.at[2 * side]))
        own.append(pltpu.make_async_copy(frac, F.at[side, 4:20, 8:40, :], in_sem.at[2 * side + 1]))
    for c in own:
        c.start()

    barrier = pltpu.get_barrier_semaphore()
    for off in everyone:
        pl.semaphore_signal(barrier, inc=1, device_id=place(*off), device_id_type=MESH)
    pl.semaphore_wait(barrier, len(everyone))

    low = 12 * (1 - gz)
    copies = {}
    count = [0]

    def start(key, src, dst, off):
        k = count[0]
        count[0] += 1
        c = pltpu.make_async_remote_copy(
            src_ref=src, dst_ref=dst, send_sem=send.at[k], recv_sem=recv.at[k], device_id=place(*off),
            device_id_type=MESH,
        )
        c.start()
        copies[key] = c

    start("z", vel.at[:, pl.ds(low, 4)], RZ, (0, 0, 1))
    start("zf", frac.at[pl.ds(low, 4)], RZF, (0, 0, 1))
    for c in own:
        c.wait()

    def pack_rows(g, _):
        for dd in range(4):
            for c in range(3):
                at = 10 * dd + 3 * c
                QU[g, at : at + 3, :] = T[1, c, 4 + 4 * g + dd, 37:40, :]
                QD[g, at : at + 3, :] = T[1, c, 4 + 4 * g + dd, 8:11, :]
            at = 10 * dd + 9
            QU[g, at : at + 1, :] = F[1, 4 + 4 * g + dd, 39:40, :]
            QD[g, at : at + 1, :] = F[1, 4 + 4 * g + dd, 8:9, :]
        return 0

    lax.fori_loop(0, 4, pack_rows, 0)
    for dx, src, dst in ((1, QU, RQL), (-1, QD, RQH)):
        start((dx, 0, 0), src, dst.at[1:5], (dx, 0, 0))
        start((dx, 0, 1), src.at[3 * (1 - gz)], dst.at[5 * gz], (dx, 0, 1))

    lane = lanes_of((8, 128))
    spot = lane // 8
    first = (lane % 8) < 4

    def pack_lanes(t, _):
        rows = pl.ds(pl.multiple_of(8 + 8 * t, 8), 8)
        both = []
        for g in range(4):
            acc = None
            for i in range(16):
                c, d = i // 4, 4 + 4 * g + i % 4
                v = turn(T[1, c, d, rows, :] if c < 3 else F[1, d, rows, :], 8 * i + 4)
                acc = v if i == 0 else jnp.where(spot == i, v, acc)
            both.append(acc)
        for h in range(2):
            a, b = both[2 * h], both[2 * h + 1]
            PL[h, t] = jnp.where(first, a, turn(b, 4))
            PR[h, t] = jnp.where(first, turn(a, -4), b)
        return 0

    lax.fori_loop(0, 4, pack_lanes, 0)
    for dy, src, dst in ((1, PL, RL), (-1, PR, RR)):
        for dx in (0, 1, -1):
            ts, td = {0: (slice(0, 4), slice(1, 5)), 1: (3, 0), -1: (0, 5)}[dx]
            start((dx, dy, 0), src.at[:, ts], dst.at[1:3, td], (dx, dy, 0))
            start((dx, dy, 1), src.at[1 - gz, ts], dst.at[3 * gz, td], (dx, dy, 1))

    RQL[5 * gz] = jnp.zeros((40, 128), F32)
    RQH[5 * gz] = jnp.zeros((40, 128), F32)
    RL[3 * gz] = jnp.zeros((6, 8, 128), F32)
    RR[3 * gz] = jnp.zeros((6, 8, 128), F32)
    blank = jnp.zeros((4, 32, 128), F32)
    for side in (0, 1):
        for c in range(3):
            T[side, c, pl.ds(20 * gz, 4), 8:40, :] = blank
        F[side, pl.ds(20 * gz, 4), 8:40, :] = blank
    copies["z"].wait()
    copies["zf"].wait()
    for side in (0, 1):
        for c in range(3):
            T[side, c, pl.ds(20 * (1 - gz), 4), 8:40, :] = RZ[c]
        F[side, pl.ds(20 * (1 - gz), 4), 8:40, :] = RZF[...]

    in_low, in_high = (gx > 0).astype(F32), (gx < 15).astype(F32)
    in_left, in_right = (gy > 0).astype(F32), (gy < 7).astype(F32)
    for dx, src, to, here in ((1, RQL, 5, in_low), (-1, RQH, 40, in_high)):
        copies[(dx, 0, 0)].wait()
        copies[(dx, 0, 1)].wait()

        def unpack_rows(g, _):
            for dd in range(4):
                for c in range(3):
                    at = 10 * dd + 3 * c
                    v = src[g, at : at + 3, :] * here
                    T[0, c, 4 * g + dd, to : to + 3, :] = v
                    T[1, c, 4 * g + dd, to : to + 3, :] = v
                at = 10 * dd + 9
                v = src[g, at : at + 1, :] * here
                one = 7 if to == 5 else 40
                F[0, 4 * g + dd, one : one + 1, :] = v
                F[1, 4 * g + dd, one : one + 1, :] = v
            return 0

        lax.fori_loop(0, 6, unpack_rows, 0)

    for dy in (1, -1):
        for dx in (0, 1, -1):
            copies[(dx, dy, 0)].wait()
            copies[(dx, dy, 1)].wait()

    outer_left, outer_right = lane >= 96, lane < 32

    def unpack_lanes(t, _):
        rows = pl.ds(pl.multiple_of(8 * t, 8), 8)
        here = jnp.where(t == 0, in_low, jnp.where(t == 5, in_high, 1.0))
        left, right = in_left * here, in_right * here
        for s in range(4):
            a, b = RL[s, t] * left, RR[s, t] * right
            for part in (0, 1):
                g = 2 * s - 1 + part
                if g < 0 or g > 5:
                    continue
                v = jnp.where(first, a, turn(b, 4)) if part == 0 else jnp.where(first, turn(a, -4), b)
                for i in range(16):
                    c, d = i // 4, 4 * g + i % 4
                    if d in (0, 23):
                        continue
                    w = turn(v, 124 - 8 * i)
                    if c < 3:
                        T[0, c, d, rows, :] = jnp.where(outer_left, w, T[0, c, d, rows, :])
                        T[1, c, d, rows, :] = jnp.where(outer_right, w, T[1, c, d, rows, :])
                    else:
                        F[0, d, rows, :] = jnp.where(outer_left, w, F[0, d, rows, :])
                        F[1, d, rows, :] = jnp.where(outer_right, w, F[1, d, rows, :])
        return 0

    lax.fori_loop(0, 6, unpack_lanes, 0)

    wide = lanes_of((32, 128))
    right_half = wide >= 64
    head, tail = wide == 0, wide == 127

    def flux_of(speed, below, above):
        return jnp.maximum(speed, 0.0) * below + jnp.minimum(speed, 0.0) * above

    def swept(q, flux_low, flux_high, speed_low, speed_high):
        return q - (flux_high - flux_low) + q * (speed_high - speed_low)

    def two(read):
        a, b = read(0), read(1)
        return jnp.where(right_half, b, a), jnp.where(right_half, a, b)

    def sweep_xy(k, _):
        d = 3 + k
        q3 = [two(lambda s, o=o: F[s, d, 7 + o : 39 + o, :]) for o in range(3)]
        u3 = [two(lambda s, o=o: T[s, 1, d, 7 + o : 39 + o, :]) for o in range(3)]
        done = []
        for which in (0, 1):
            q, u = [x[which] for x in q3], [x[which] for x in u3]
            lo, hi = 0.5 * (u[0] + u[1]), 0.5 * (u[1] + u[2])
            done.append(swept(q[1], flux_of(lo, q[0], q[1]), flux_of(hi, q[1], q[2]), lo, hi))
        q, qh = done
        u, uh = two(lambda s: T[s, 2, d, 8:40, :])
        ql, ul = turn(jnp.where(tail, qh, q), 1), turn(jnp.where(tail, uh, u), 1)
        qr, ur = turn(jnp.where(head, qh, q), -1), turn(jnp.where(head, uh, u), -1)
        lo, hi = 0.5 * (ul + u), 0.5 * (u + ur)
        SQ[k] = swept(q, flux_of(lo, ql, q), flux_of(hi, q, qr), lo, hi)
        return 0

    lax.fori_loop(0, 18, sweep_xy, 0)

    HB[...] = jnp.zeros((32, 128), F32)

    def sweep_z(k, _):
        q = [SQ[k + o] for o in range(3)]
        u = [two(lambda s, o=o: T[s, 0, 3 + k + o, 8:40, :])[0] for o in range(3)]
        lo, hi = 0.5 * (u[0] + u[1]), 0.5 * (u[1] + u[2])
        new = swept(q[1], flux_of(lo, q[0], q[1]), flux_of(hi, q[1], q[2]), lo, hi)
        fout[k] = new
        HB[...] += new
        return 0

    lax.fori_loop(0, 16, sweep_z, 0)

    heights = []
    for j, (dx, dy, dz) in enumerate(everyone):
        rows = {0: slice(0, 32), 1: slice(24, 32), -1: slice(0, 8)}[dx]
        if dx == 0 and dy == 0:
            dst = HP
        elif dy == 0:
            dst = HX.at[dz, (dx < 0) * 1]
        elif dx == 0:
            dst = HY.at[dz, (dy < 0) * 1]
        else:
            dst = HC.at[dz, (dx < 0) * 2 + (dy < 0) * 1]
        c = pltpu.make_async_remote_copy(
            src_ref=HB.at[rows], dst_ref=dst, send_sem=hsend.at[j], recv_sem=hrecv.at[j],
            device_id=place(dx, dy, dz), device_id_type=MESH,
        )
        c.start()
        heights.append(c)
    for c in heights:
        c.wait()

    HS[0, 8:40] = HB[...] + HP[...]
    HS[0, 0:8] = (HX[0, 0] + HX[1, 0]) * in_low
    HS[0, 40:48] = (HX[0, 1] + HX[1, 1]) * in_high
    HS[1, 8:40] = jnp.where(
        right_half, (HY[0, 0] + HY[1, 0]) * in_left, (HY[0, 1] + HY[1, 1]) * in_right
    )
    for x, at, here in ((0, 0, in_low), (1, 40, in_high)):
        HS[1, at : at + 8] = jnp.where(
            lane >= 64,
            (HC[0, 2 * x] + HC[1, 2 * x]) * (in_left * here),
            (HC[0, 2 * x + 1] + HC[1, 2 * x + 1]) * (in_right * here),
        )
    all_lanes = lanes_of((48, 128))
    h, hh = HS[0], HS[1]
    HN[...] = turn(jnp.where(all_lanes == 0, hh, h), -1)
    HM[...] = turn(jnp.where(all_lanes == 127, hh, h), 1)
    middle, east, west = HS[0, 8:40], HS[0, 9:41], HS[0, 7:39]
    north, south = HN[8:40], HM[8:40]
    slope_x, slope_y = 0.5 * (east - west), 0.5 * (north - south)
    bend_xx = east - 2.0 * middle + west
    bend_yy = north - 2.0 * middle + south
    bend_xy = 0.25 * (HN[9:41] - HM[9:41] - HN[7:39] + HM[7:39])
    metric = 1.0 + slope_x * slope_x + slope_y * slope_y
    top = (
        bend_xx * (1.0 + slope_y * slope_y) + bend_yy * (1.0 + slope_x * slope_x)
        - 2.0 * slope_x * slope_y * bend_xy
    )
    curv[...] = top / (metric * jnp.sqrt(metric))


def along(x, idx, axis):
    return jnp.take_along_axis(x, idx, axis=axis, mode="promise_in_bounds")


GROUP = 16


def particle_kernel(
    cen, counts, T, fin, cin, points, active, start, mass, inertia,
    fout, cout, mult, motion, ED, ER, EC, A, AT, RM, sem,
):
    passed = [pltpu.make_async_copy(fin, fout, sem.at[0]), pltpu.make_async_copy(cin, cout, sem.at[1])]
    for c in passed:
        c.start()
    code = points[...]
    ed = (code * 1338) >> 16
    rest = code - ed * 49
    er = (rest * 9363) >> 16
    ED[...] = ed
    ER[...] = er
    EC[...] = rest - er * 7
    A[...] = jnp.zeros((128, 128), F32)
    A[0:6, :] = start[...]
    A[6:7, :] = mass[...]
    A[7:8, :] = inertia[...]
    AT[...] = A[...].T
    owned = counts[0]
    lane = lanes_of((GROUP, 128))
    row8 = lax.broadcasted_iota(I32, (8, 128), 0)

    def cross(a, b):
        return [a[1] * b[2] - a[2] * b[1], a[2] * b[0] - a[0] * b[2], a[0] * b[1] - a[1] * b[0]]

    def group(g, _):
        base = pl.multiple_of(g * GROUP, GROUP)
        tiles = [[None] * (GROUP // 8) for _ in range(3)]
        for s in range(GROUP):
            q = base + s
            d0 = cen[0, q] - 2
            r0 = cen[1, q] + 2
            jc = cen[2, q] - 3
            side = (jc >= 64).astype(I32)
            e_d = jnp.broadcast_to(ED[pl.ds(q, 1), :], (8, 128))
            e_r = jnp.broadcast_to(ER[pl.ds(q, 1), :], (8, 128))
            idx = (jnp.broadcast_to(EC[pl.ds(q, 1), :], (8, 128)) + (jc - 3)) & 127
            picks = [e_d == k for k in range(1, 7)]
            for c in range(3):
                acc = None
                for k in range(7):
                    v = along(T[side, c, d0 + k, pl.ds(r0, 8), :], idx, 1)
                    acc = v if k == 0 else jnp.where(picks[k - 1], v, acc)
                res = along(acc, e_r, 0)
                old = tiles[c][s // 8]
                tiles[c][s // 8] = res if s % 8 == 0 else jnp.where(row8 == s % 8, res, old)
        sampled = [jnp.concatenate(t, axis=0) for t in tiles]
        rows = pl.ds(base, GROUP)
        offsets = [(e[rows, :] - 3).astype(F32) for e in (ED, ER, EC)]
        alive = ((lax.broadcasted_iota(I32, (GROUP, 128), 0) + base) < owned).astype(F32)
        weight = active[rows, :].astype(F32) * alive
        columns = AT[rows, :]
        column = [columns[:, k : k + 1] for k in range(8)]
        linear, angular = column[0:3], column[3:6]
        m = None
        for it in range(2):
            spin = cross(angular, offsets)
            moving = [linear[k] + spin[k] for k in range(3)]
            if it == 0:
                m = [(sampled[k] - moving[k]) * weight for k in range(3)]
            else:
                m = [(m[k] + (sampled[k] - 0.5 * m[k] - moving[k])) * weight for k in range(3)]
            torque = cross(offsets, m)
            linear = [column[k] + column[6] * jnp.sum(m[k], axis=1, keepdims=True) for k in range(3)]
            angular = [column[3 + k] + column[7] * jnp.sum(torque[k], axis=1, keepdims=True) for k in range(3)]
        for k in range(3):
            mult[k, rows, :] = m[k]
        out = jnp.zeros((GROUP, 128), F32)
        for k in range(6):
            out = jnp.where(lane == k, (linear + angular)[k], out)
        RM[rows, :] = out * alive
        return 0

    lax.fori_loop(0, 128 // GROUP, group, 0)
    motion[...] = RM[...].T[0:6, :]
    for c in passed:
        c.wait()


def body(fraction, velocity, centres, points, active_points, counts, rigid_start, mass, inertia):
    vmem, smem = pl.BlockSpec(memory_space=pltpu.VMEM), pl.BlockSpec(memory_space=pltpu.SMEM)
    anywhere = pl.BlockSpec(memory_space=pl.ANY)

    def f32(*shape):
        return jax.ShapeDtypeStruct(shape, F32)

    def room(*shape):
        return pltpu.VMEM(shape, F32)

    table, swept, curvature = pl.pallas_call(
        halo_kernel,
        out_shape=(f32(2, 3, 24, 48, 128), f32(16, 32, 128), f32(32, 128)),
        in_specs=[anywhere] * 2,
        out_specs=(vmem, vmem, vmem),
        scratch_shapes=[
            room(2, 24, 48, 128),
            room(4, 40, 128), room(4, 40, 128), room(6, 40, 128), room(6, 40, 128),
            room(2, 4, 8, 128), room(2, 4, 8, 128), room(4, 6, 8, 128), room(4, 6, 8, 128),
            room(3, 4, 32, 128), room(4, 32, 128), room(18, 32, 128),
            room(32, 128), room(32, 128), room(2, 2, 8, 128), room(2, 2, 32, 128), room(2, 4, 8, 128),
            room(2, 48, 128), room(48, 128), room(48, 128),
            pltpu.SemaphoreType.DMA((4,)),
            pltpu.SemaphoreType.DMA((18,)), pltpu.SemaphoreType.DMA((18,)),
            pltpu.SemaphoreType.DMA((17,)), pltpu.SemaphoreType.DMA((17,)),
        ],
        compiler_params=pltpu.CompilerParams(
            collective_id=0, has_side_effects=True, vmem_limit_bytes=40 << 20
        ),
        name="halo_and_sweeps",
    )(fraction, velocity)
    return pl.pallas_call(
        particle_kernel,
        out_shape=(f32(16, 32, 128), f32(32, 128), f32(3, 128, 128), f32(6, 128)),
        in_specs=[smem, smem, vmem, anywhere, anywhere] + [vmem] * 5,
        out_specs=(anywhere, anywhere, vmem, vmem),
        scratch_shapes=[pltpu.VMEM((128, 128), I32)] * 3 + [room(128, 128)] * 3 + [pltpu.SemaphoreType.DMA((2,))],
        compiler_params=pltpu.CompilerParams(vmem_limit_bytes=40 << 20),
        name="particles",
    )(
        centres, counts, table, swept, curvature, points, active_points, rigid_start,
        mass.reshape(1, 128), inertia.reshape(1, 128),
    )


def solution(mesh):
    bricks = ("gx", "gy", "gz")
    placed = (
        P("gz", "gx", "gy"), P(None, "gz", "gx", "gy"), P(None, bricks), P(bricks, None), P(bricks, None),
        P(bricks), P(None, bricks), P(bricks), P(bricks),
    )
    return jax.shard_map(
        body, mesh=mesh, in_specs=placed,
        out_specs=(P("gz", "gx", "gy"), P("gx", "gy"), P(None, bricks, None), P(None, bricks)),
        check_vma=False,
    )
```

time: 237 us -> 49.3 us (0.21)
  the two profiles are of different devices: /device:TPU:57 before, /device:TPU:1 now
where the time goes in v1:
time: 49.3 us; the launch traced here: 49 us
  Pallas kernels  41.2 us (84%)
  local copies, waits for them, and re-layouts  6.43 us (13%)
  between operations  1.31 us (3%)
    pallas_call x1, Pallas kernels, body(): pl.pallas_call(halo_kernel, out_shape=(f32(2, 3, 24, 48, 128), f32(16, 32...  29.1 us
    pallas_call x1, Pallas kernels, body(): pl.pallas_call(particle_kernel, out_shape=(f32(16, 32, 128), f32(32, 128)...  12.1 us
    unnamed x16, local copies, waits for them, and re-layouts  6.43 us

profile of v1, /device:TPU:1, one launch (start us, length us, event | category | flops | bytes accessed | tf_op | source)
XLA Modules:
  0.0 49.0 jit_solution(15388382727640194165)
XLA Ops:
  1.3 0.0 copy-start
  1.3 1.1 %copy-done = f32[3,16,32,128]{3,2,1,0:T(8,128)S(1)} copy-done((f32[3,16,32,128]{3,2,1,0:T(8,128)S(1)}, f32[3,16,32,128]{3,2,1,0:T(8,128)}, u32[]{:S(2)}) %copy-start) | copy-done | bytes 786456
  2.4 0.0 copy-start.1
  2.4 0.9 %copy-done.1 = f32[16,32,128]{2,1,0:T(8,128)S(1)} copy-done((f32[16,32,128]{2,1,0:T(8,128)S(1)}, f32[16,32,128]{2,1,0:T(8,128)}, u32[]{:S(2)}) %copy-start.1) | copy-done | bytes 262168
  3.4 29.1 %halo_and_sweeps.1 = (f32[2,3,24,48,128]{4,3,2,1,0:T(8,128)S(1)}, f32[16,32,128]{2,1,0:T(8,128)S(1)}, f32[32,128]{1,0:T(8,128)S(1)}) custom-call(f32[16,32,128]{2,1,0:T(8,128)S(1)} %copy-done.1, f32[3,16,32,128]{3,2,1,0:T(8,128)S(1)} %copy-done), custom_call_target="tpu_custom_call" | custom-call | tf_op jit(solution)/shard_map/halo_and_sweeps/pallas_call | solution.py:373
  32.5 0.0 copy-start.2
  32.5 0.8 %copy-done.2 = s32[128,128]{1,0:T(8,128)S(1)} copy-done((s32[128,128]{1,0:T(8,128)S(1)}, s32[128,128]{1,0:T(8,128)}, u32[]{:S(2)}) %copy-start.2) | copy-done | bytes 65560
  33.4 0.0 copy-start.3
  33.4 0.8 %copy-done.3 = s32[128,128]{1,0:T(8,128)S(1)} copy-done((s32[128,128]{1,0:T(8,128)S(1)}, s32[128,128]{1,0:T(8,128)}, u32[]{:S(2)}) %copy-start.3) | copy-done | bytes 65560
  34.2 0.0 copy-start.4
  34.2 0.7 %copy-done.4 = f32[6,128]{1,0:T(8,128)S(1)} copy-done((f32[6,128]{1,0:T(8,128)S(1)}, f32[6,128]{1,0:T(8,128)}, u32[]{:S(2)}) %copy-start.4) | copy-done | bytes 3096
  34.9 0.0 copy-start.5
  34.9 0.7 %copy-done.5 = s32[3,128]{1,0:T(4,128)S(1)} copy-done((s32[3,128]{1,0:T(4,128)S(1)}, s32[3,128]{1,0:T(4,128)}, u32[]{:S(2)}) %copy-start.5) | copy-done | bytes 1560
  35.6 0.0 copy-start.6
  35.6 0.7 %copy-done.6 = f32[128]{0:T(128)S(1)} copy-done((f32[128]{0:T(128)S(1)}, f32[128]{0:T(128)}, u32[]{:S(2)}) %copy-start.6) | copy-done | bytes 536
  36.2 0.0 copy-start.7
  36.2 0.7 %copy-done.7 = f32[128]{0:T(128)S(1)} copy-done((f32[128]{0:T(128)S(1)}, f32[128]{0:T(128)}, u32[]{:S(2)}) %copy-start.7) | copy-done | bytes 536
  36.9 12.1 %particles.1 = (f32[16,32,128]{2,1,0:T(8,128)}, f32[32,128]{1,0:T(8,128)}, f32[3,128,128]{2,1,0:T(8,128)}, f32[6,128]{1,0:T(8,128)}) custom-call(s32[3,128]{1,0:T(4,128)S(1)} %copy-done.5, s32[1]{0:T(128)S(6)} %copy.13.counts, f32[2,3,24,48,128]{4,3,2,1,0:T(8,128)S(1)} %get-tuple-element.7.T, f32[16,32,128]{2,1,0:T(8,128)S(1)} %get-tuple-element.8.fin, ...), custom_call_target="tpu_custom_call" | custom-call | tf_op jit(solution)/shard_map/particles/pallas_call | solution.py:394
Async XLA Ops:
  1.3 1.1 %copy-start = (f32[3,16,32,128]{3,2,1,0:T(8,128)S(1)}, f32[3,16,32,128]{3,2,1,0:T(8,128)}, u32[]{:S(2)}) copy-start(f32[3,16,32,128]{3,2,1,0:T(8,128)} %vel.1) | copy-start | bytes 2359300
  2.4 0.9 %copy-start.1 = (f32[16,32,128]{2,1,0:T(8,128)S(1)}, f32[16,32,128]{2,1,0:T(8,128)}, u32[]{:S(2)}) copy-start(f32[16,32,128]{2,1,0:T(8,128)} %frac.1) | copy-start | bytes 786436
  32.5 0.8 %copy-start.2 = (s32[128,128]{1,0:T(8,128)S(1)}, s32[128,128]{1,0:T(8,128)}, u32[]{:S(2)}) copy-start(s32[128,128]{1,0:T(8,128)} %points.1) | copy-start | bytes 196612
  33.4 0.8 %copy-start.3 = (s32[128,128]{1,0:T(8,128)S(1)}, s32[128,128]{1,0:T(8,128)}, u32[]{:S(2)}) copy-start(s32[128,128]{1,0:T(8,128)} %active.1) | copy-start | bytes 196612
  34.2 0.7 %copy-start.4 = (f32[6,128]{1,0:T(8,128)S(1)}, f32[6,128]{1,0:T(8,128)}, u32[]{:S(2)}) copy-start(f32[6,128]{1,0:T(8,128)} %start.1) | copy-start | bytes 9220
  34.9 0.7 %copy-start.5 = (s32[3,128]{1,0:T(4,128)S(1)}, s32[3,128]{1,0:T(4,128)}, u32[]{:S(2)}) copy-start(s32[3,128]{1,0:T(4,128)} %cen.1) | copy-start | bytes 4612
  35.6 0.7 %copy-start.6 = (f32[128]{0:T(128)S(1)}, f32[128]{0:T(128)}, u32[]{:S(2)}) copy-start(f32[128]{0:T(128)} %param.16) | copy-start | bytes 1540
  36.2 0.7 %copy-start.7 = (f32[128]{0:T(128)S(1)}, f32[128]{0:T(128)}, u32[]{:S(2)}) copy-start(f32[128]{0:T(128)} %param.17) | copy-start | bytes 1540

commit v2 on v1

--- a/solution.py
+++ b/solution.py
@@ -6,6 +6,7 @@
 from jax.sharding import PartitionSpec as P
 
 MESH = pl.DeviceIdType.MESH
+GROUP = 16
 F32 = jnp.float32
 I32 = jnp.int32
 
@@ -21,8 +22,18 @@
     return pltpu.roll(x, by, x.ndim - 1) if by else x
 
 
-def halo_kernel(
-    frac, vel, T, fout, curv,
+def along(x, idx, axis):
+    return jnp.take_along_axis(x, idx, axis=axis, mode="promise_in_bounds")
+
+
+def cross(a, b):
+    return [a[1] * b[2] - a[2] * b[1], a[2] * b[0] - a[0] * b[2], a[0] * b[1] - a[1] * b[0]]
+
+
+def brick_kernel(
+    frac, vel, cen_in, counts_in, points_in, active_in, start_in, mass_in, inertia_in,
+    fout, curv, mult, motion,
+    cen, counts, points, active, rigid, mass, inertia, ED, ER, EC, WT, A, AT, SM, CB, RM, T,
     F, QU, QD, RQL, RQH, PL, PR, RL, RR, RZ, RZF, SQ, HB, HP, HX, HY, HC, HS, HN, HM,
     in_sem, send, recv, hsend, hrecv,
 ):
@@ -38,11 +49,19 @@
         own.append(pltpu.make_async_copy(frac, F.at[side, 4:20, 8:40, :], in_sem.at[2 * side + 1]))
     for c in own:
         c.start()
+    small = [
+        pltpu.make_async_copy(src, dst, in_sem.at[4 + k])
+        for k, (src, dst) in enumerate((
+            (points_in, points), (active_in, active), (start_in, rigid), (mass_in, mass),
+            (inertia_in, inertia), (cen_in, cen), (counts_in, counts),
+        ))
+    ]
+    for c in small:
+        c.start()
 
     barrier = pltpu.get_barrier_semaphore()
     for off in everyone:
         pl.semaphore_signal(barrier, inc=1, device_id=place(*off), device_id_type=MESH)
-    pl.semaphore_wait(barrier, len(everyone))
 
     low = 12 * (1 - gz)
     copies = {}
@@ -58,8 +77,6 @@
         c.start()
         copies[key] = c
 
-    start("z", vel.at[:, pl.ds(low, 4)], RZ, (0, 0, 1))
-    start("zf", frac.at[pl.ds(low, 4)], RZF, (0, 0, 1))
     for c in own:
         c.wait()
 
@@ -75,9 +92,13 @@
         return 0
 
     lax.fori_loop(0, 4, pack_rows, 0)
+    pl.semaphore_wait(barrier, len(everyone))
     for dx, src, dst in ((1, QU, RQL), (-1, QD, RQH)):
         start((dx, 0, 0), src, dst.at[1:5], (dx, 0, 0))
         start((dx, 0, 1), src.at[3 * (1 - gz)], dst.at[5 * gz], (dx, 0, 1))
+
+    start("z", vel.at[:, pl.ds(low, 4)], RZ, (0, 0, 1))
+    start("zf", frac.at[pl.ds(low, 4)], RZF, (0, 0, 1))
 
     lane = lanes_of((8, 128))
     spot = lane // 8
@@ -115,6 +136,61 @@
         for c in range(3):
             T[side, c, pl.ds(20 * gz, 4), 8:40, :] = blank
         F[side, pl.ds(20 * gz, 4), 8:40, :] = blank
+
+    for c in small:
+        c.wait()
+    A[...] = jnp.zeros((128, 128), F32)
+    A[0:6, :] = rigid[...]
+    A[6:7, :] = mass[...]
+    A[7:8, :] = inertia[...]
+    AT[...] = A[...].T
+    owned = counts[0]
+    ones = jnp.ones((256, 128), jnp.bfloat16)
+
+    def total(x):
+        return jnp.dot(x.astype(jnp.bfloat16), ones[:128], preferred_element_type=F32)
+
+    def prepare(k, _):
+        base = pl.multiple_of(32 * k, 32)
+        rows = pl.ds(base, 32)
+        code = points[rows, :]
+        ed = (code * 1338) >> 16
+        rest = code - ed * 49
+        er = (rest * 9363) >> 16
+        ec = rest - er * 7
+        ED[rows, :] = ed
+        ER[rows, :] = er
+        EC[rows, :] = ec
+        alive = ((lax.broadcasted_iota(I32, (32, 128), 0) + base) < owned).astype(F32)
+        w = active[rows, :].astype(F32) * alive
+        WT[rows, :] = w
+        e = [(x - 3).astype(F32) for x in (ed, er, ec)]
+        we = [w * x for x in e]
+        m0 = total(w)
+        m1 = [total(x) for x in we]
+        m2 = {(i, j): total(we[i] * e[j]) for i in range(3) for j in range(i, 3)}
+        J = [m2[(1, 1)] + m2[(2, 2)], m2[(0, 0)] + m2[(2, 2)], m2[(0, 0)] + m2[(1, 1)]]
+        columns = AT[rows, :]
+        column = [jnp.broadcast_to(columns[:, c : c + 1], (32, 128)) for c in range(8)]
+        for c, x in enumerate(column + [m0] + m1 + J + [m2[(0, 1)], m2[(0, 2)], m2[(1, 2)]]):
+            CB[c, rows, :] = x
+        force, torque = pull(column[0:3], column[3:6], m0, m1, J, m2[(0, 1)], m2[(0, 2)], m2[(1, 2)])
+        for c, x in enumerate(force + torque):
+            CB[18 + c, rows, :] = x
+        return 0
+
+    def pull(linear, angular, m0, m1, J, xy, xz, yz):
+        turned = cross(angular, m1)
+        force = [m0 * linear[c] + turned[c] for c in range(3)]
+        lever = cross(m1, linear)
+        torque = [
+            lever[0] + (J[0] * angular[0] - xy * angular[1] - xz * angular[2]),
+            lever[1] + (J[1] * angular[1] - xy * angular[0] - yz * angular[2]),
+            lever[2] + (J[2] * angular[2] - xz * angular[0] - yz * angular[1]),
+        ]
+        return force, torque
+
+    lax.fori_loop(0, 4, prepare, 0)
     copies["z"].wait()
     copies["zf"].wait()
     for side in (0, 1):
@@ -240,6 +316,71 @@
         )
         c.start()
         heights.append(c)
+
+    row8 = lax.broadcasted_iota(I32, (8, 128), 0)
+
+    def sample(g, _):
+        base = pl.multiple_of(g * GROUP, GROUP)
+        tiles = [[None] * (GROUP // 8) for _ in range(3)]
+        for s in range(GROUP):
+            q = base + s
+            d0 = jnp.clip(cen[0, q] - 2, 1, 16)
+            r0 = jnp.clip(cen[1, q] + 2, 5, 36)
+            jc = cen[2, q] - 3
+            side = (jc >= 64).astype(I32)
+            e_d = jnp.broadcast_to(ED[pl.ds(q, 1), :], (8, 128))
+            e_r = jnp.broadcast_to(ER[pl.ds(q, 1), :], (8, 128))
+            idx = (jnp.broadcast_to(EC[pl.ds(q, 1), :], (8, 128)) + (jc - 3)) & 127
+            picks = [e_d == k for k in range(1, 7)]
+            for c in range(3):
+                acc = None
+                for k in range(7):
+                    v = along(T[side, c, d0 + k, pl.ds(r0, 8), :], idx, 1)
+                    acc = v if k == 0 else jnp.where(picks[k - 1], v, acc)
+                res = along(acc, e_r, 0)
+                old = tiles[c][s // 8]
+                tiles[c][s // 8] = res if s % 8 == 0 else jnp.where(row8 == s % 8, res, old)
+        for c in range(3):
+            SM[c, pl.ds(base, GROUP), :] = jnp.concatenate(tiles[c], axis=0)
+        return 0
+
+    lax.fori_loop(0, 128 // GROUP, sample, 0)
+
+    def total_of(x):
+        high = x.astype(jnp.bfloat16)
+        rest = (x - high.astype(F32)).astype(jnp.bfloat16)
+        return jnp.dot(jnp.concatenate([high, rest], axis=1), ones, preferred_element_type=F32)
+
+    def iterate(k, _):
+        rows = pl.ds(pl.multiple_of(32 * k, 32), 32)
+        s = [SM[c, rows, :] for c in range(3)]
+        w = WT[rows, :]
+        e = [(x[rows, :] - 3).astype(F32) for x in (ED, ER, EC)]
+        ws = [w * x for x in s]
+        S = [total_of(x) for x in ws]
+        Q = [total_of(x) for x in cross(e, ws)]
+        n = [CB[c, rows, :] for c in range(24)]
+        linear, angular, force, torque = n[0:3], n[3:6], n[18:21], n[21:24]
+        linear1 = [linear[c] + n[6] * (S[c] - force[c]) for c in range(3)]
+        angular1 = [angular[c] + n[7] * (Q[c] - torque[c]) for c in range(3)]
+        force1, torque1 = pull(linear1, angular1, n[8], n[9:12], n[12:15], n[15], n[16], n[17])
+        last = [linear[c] + n[6] * (1.5 * S[c] - 0.5 * force[c] - force1[c]) for c in range(3)]
+        last += [angular[c] + n[7] * (1.5 * Q[c] - 0.5 * torque[c] - torque1[c]) for c in range(3)]
+        both = [0.5 * linear[c] + linear1[c] for c in range(3)]
+        spin = cross([0.5 * angular[c] + angular1[c] for c in range(3)], e)
+        for c in range(3):
+            mult[c, rows, :] = 1.5 * ws[c] - w * (both[c] + spin[c])
+        lanes = lanes_of((32, 128))
+        out = jnp.zeros((32, 128), F32)
+        for c in range(6):
+            out = jnp.where(lanes == c, last[c], out)
+        alive = ((lax.broadcasted_iota(I32, (32, 128), 0) + 32 * k) < owned).astype(F32)
+        RM[rows, :] = out * alive
+        return 0
+
+    lax.fori_loop(0, 4, iterate, 0)
+    motion[...] = RM[...].T[0:6, :]
+
     for c in heights:
         c.wait()
 
@@ -273,136 +414,62 @@
     curv[...] = top / (metric * jnp.sqrt(metric))
 
 
-def along(x, idx, axis):
-    return jnp.take_along_axis(x, idx, axis=axis, mode="promise_in_bounds")
-
-
-GROUP = 16
-
-
-def particle_kernel(
-    cen, counts, T, fin, cin, points, active, start, mass, inertia,
-    fout, cout, mult, motion, ED, ER, EC, A, AT, RM, sem,
-):
-    passed = [pltpu.make_async_copy(fin, fout, sem.at[0]), pltpu.make_async_copy(cin, cout, sem.at[1])]
-    for c in passed:
+def pass_kernel(*refs):
+    n = (len(refs) - 1) // 2
+    moves = [pltpu.make_async_copy(refs[k], refs[n + k], refs[-1].at[k]) for k in range(n)]
+    for c in moves:
         c.start()
-    code = points[...]
-    ed = (code * 1338) >> 16
-    rest = code - ed * 49
-    er = (rest * 9363) >> 16
-    ED[...] = ed
-    ER[...] = er
-    EC[...] = rest - er * 7
-    A[...] = jnp.zeros((128, 128), F32)
-    A[0:6, :] = start[...]
-    A[6:7, :] = mass[...]
-    A[7:8, :] = inertia[...]
-    AT[...] = A[...].T
-    owned = counts[0]
-    lane = lanes_of((GROUP, 128))
-    row8 = lax.broadcasted_iota(I32, (8, 128), 0)
-
-    def cross(a, b):
-        return [a[1] * b[2] - a[2] * b[1], a[2] * b[0] - a[0] * b[2], a[0] * b[1] - a[1] * b[0]]
-
-    def group(g, _):
-        base = pl.multiple_of(g * GROUP, GROUP)
-        tiles = [[None] * (GROUP // 8) for _ in range(3)]
-        for s in range(GROUP):
-            q = base + s
-            d0 = cen[0, q] - 2
-            r0 = cen[1, q] + 2
-            jc = cen[2, q] - 3
-            side = (jc >= 64).astype(I32)
-            e_d = jnp.broadcast_to(ED[pl.ds(q, 1), :], (8, 128))
-            e_r = jnp.broadcast_to(ER[pl.ds(q, 1), :], (8, 128))
-            idx = (jnp.broadcast_to(EC[pl.ds(q, 1), :], (8, 128)) + (jc - 3)) & 127
-            picks = [e_d == k for k in range(1, 7)]
-            for c in range(3):
-                acc = None
-                for k in range(7):
-                    v = along(T[side, c, d0 + k, pl.ds(r0, 8), :], idx, 1)
-                    acc = v if k == 0 else jnp.where(picks[k - 1], v, acc)
-                res = along(acc, e_r, 0)
-                old = tiles[c][s // 8]
-                tiles[c][s // 8] = res if s % 8 == 0 else jnp.where(row8 == s % 8, res, old)
-        sampled = [jnp.concatenate(t, axis=0) for t in tiles]
-        rows = pl.ds(base, GROUP)
-        offsets = [(e[rows, :] - 3).astype(F32) for e in (ED, ER, EC)]
-        alive = ((lax.broadcasted_iota(I32, (GROUP, 128), 0) + base) < owned).astype(F32)
-        weight = active[rows, :].astype(F32) * alive
-        columns = AT[rows, :]
-        column = [columns[:, k : k + 1] for k in range(8)]
-        linear, angular = column[0:3], column[3:6]
-        m = None
-        for it in range(2):
-            spin = cross(angular, offsets)
-            moving = [linear[k] + spin[k] for k in range(3)]
-            if it == 0:
-                m = [(sampled[k] - moving[k]) * weight for k in range(3)]
-            else:
-                m = [(m[k] + (sampled[k] - 0.5 * m[k] - moving[k])) * weight for k in range(3)]
-            torque = cross(offsets, m)
-            linear = [column[k] + column[6] * jnp.sum(m[k], axis=1, keepdims=True) for k in range(3)]
-            angular = [column[3 + k] + column[7] * jnp.sum(torque[k], axis=1, keepdims=True) for k in range(3)]
-        for k in range(3):
-            mult[k, rows, :] = m[k]
-        out = jnp.zeros((GROUP, 128), F32)
-        for k in range(6):
-            out = jnp.where(lane == k, (linear + angular)[k], out)
-        RM[rows, :] = out * alive
-        return 0
-
-    lax.fori_loop(0, 128 // GROUP, group, 0)
-    motion[...] = RM[...].T[0:6, :]
-    for c in passed:
+    for c in moves:
         c.wait()
 
 
 def body(fraction, velocity, centres, points, active_points, counts, rigid_start, mass, inertia):
-    vmem, smem = pl.BlockSpec(memory_space=pltpu.VMEM), pl.BlockSpec(memory_space=pltpu.SMEM)
-    anywhere = pl.BlockSpec(memory_space=pl.ANY)
+    vmem, anywhere = pl.BlockSpec(memory_space=pltpu.VMEM), pl.BlockSpec(memory_space=pl.ANY)
+    hbm = pl.BlockSpec(memory_space=pltpu.HBM)
 
     def f32(*shape):
         return jax.ShapeDtypeStruct(shape, F32)
 
-    def room(*shape):
-        return pltpu.VMEM(shape, F32)
-
-    table, swept, curvature = pl.pallas_call(
-        halo_kernel,
-        out_shape=(f32(2, 3, 24, 48, 128), f32(16, 32, 128), f32(32, 128)),
-        in_specs=[anywhere] * 2,
-        out_specs=(vmem, vmem, vmem),
+    def room(*shape, dtype=F32):
+        return pltpu.VMEM(shape, dtype)
+
+    outs = (f32(16, 32, 128), f32(32, 128), f32(3, 128, 128), f32(6, 128))
+    results = pl.pallas_call(
+        brick_kernel,
+        out_shape=outs,
+        in_specs=[hbm] * 9,
+        out_specs=(vmem,) * 4,
         scratch_shapes=[
-            room(2, 24, 48, 128),
+            pltpu.SMEM((3, 128), I32), pltpu.SMEM((1,), I32),
+            room(128, 128, dtype=I32), room(128, 128, dtype=I32), room(6, 128), room(1, 128), room(1, 128),
+            room(128, 128, dtype=I32), room(128, 128, dtype=I32), room(128, 128, dtype=I32),
+            room(128, 128), room(128, 128), room(128, 128), room(3, 128, 128), room(24, 128, 128), room(128, 128),
+            room(2, 3, 24, 48, 128), room(2, 24, 48, 128),
             room(4, 40, 128), room(4, 40, 128), room(6, 40, 128), room(6, 40, 128),
             room(2, 4, 8, 128), room(2, 4, 8, 128), room(4, 6, 8, 128), room(4, 6, 8, 128),
             room(3, 4, 32, 128), room(4, 32, 128), room(18, 32, 128),
             room(32, 128), room(32, 128), room(2, 2, 8, 128), room(2, 2, 32, 128), room(2, 4, 8, 128),
             room(2, 48, 128), room(48, 128), room(48, 128),
-            pltpu.SemaphoreType.DMA((4,)),
+            pltpu.SemaphoreType.DMA((11,)),
             pltpu.SemaphoreType.DMA((18,)), pltpu.SemaphoreType.DMA((18,)),
             pltpu.SemaphoreType.DMA((17,)), pltpu.SemaphoreType.DMA((17,)),
         ],
         compiler_params=pltpu.CompilerParams(
-            collective_id=0, has_side_effects=True, vmem_limit_bytes=40 << 20
+            collective_id=0, has_side_effects=True, vmem_limit_bytes=60 << 20
         ),
-        name="halo_and_sweeps",
-    )(fraction, velocity)
-    return pl.pallas_call(
-        particle_kernel,
-        out_shape=(f32(16, 32, 128), f32(32, 128), f32(3, 128, 128), f32(6, 128)),
-        in_specs=[smem, smem, vmem, anywhere, anywhere] + [vmem] * 5,
-        out_specs=(anywhere, anywhere, vmem, vmem),
-        scratch_shapes=[pltpu.VMEM((128, 128), I32)] * 3 + [room(128, 128)] * 3 + [pltpu.SemaphoreType.DMA((2,))],
-        compiler_params=pltpu.CompilerParams(vmem_limit_bytes=40 << 20),
-        name="particles",
+        name="brick",
     )(
-        centres, counts, table, swept, curvature, points, active_points, rigid_start,
+        fraction, velocity, centres, counts, points, active_points, rigid_start,
         mass.reshape(1, 128), inertia.reshape(1, 128),
     )
+    return pl.pallas_call(
+        pass_kernel,
+        out_shape=outs,
+        in_specs=[vmem] * 4,
+        out_specs=(hbm,) * 4,
+        scratch_shapes=[pltpu.SemaphoreType.DMA((4,))],
+        name="pass_on",
+    )(*results)
 
 
 def solution(mesh):

time: 49.3 us -> 33.1 us (0.67)
  Pallas kernels: 41.2 us -> 31.6 us
  local copies, waits for them, and re-layouts: 6.43 us -> 0 us
    pallas_call x2, Pallas kernels: 41.2 us -> 31.6 us  [the longest x1 29.8 us: body(): pl.pallas_call(brick_kernel, out_shape=outs, in_specs=[hbm] * 9, out_spec...]
    unnamed x16 -> x0, local copies, waits for them, and re-layouts: 6.43 us -> none
where the time goes in v2:
time: 33.1 us; the launch traced here: 32.9 us
  Pallas kernels  31.6 us (95%)
  between operations  1.29 us (4%)
    pallas_call x1, Pallas kernels, body(): pl.pallas_call(brick_kernel, out_shape=outs, in_specs=[hbm] * 9, out_spec...  29.8 us
    pallas_call x1, Pallas kernels, body(): pl.pallas_call(pass_kernel, out_shape=outs, in_specs=[vmem] * 4, out_spec...  1.83 us

profile of v2, /device:TPU:1, one launch (start us, length us, event | category | flops | bytes accessed | tf_op | source)
XLA Modules:
  0.0 32.9 jit_solution(5284758694803811034)
XLA Ops:
  1.3 29.8 %brick.1 = (f32[16,32,128]{2,1,0:T(8,128)}, f32[32,128]{1,0:T(8,128)}, f32[3,128,128]{2,1,0:T(8,128)}, f32[6,128]{1,0:T(8,128)}) custom-call(f32[16,32,128]{2,1,0:T(8,128)} %frac.1, f32[3,16,32,128]{3,2,1,0:T(8,128)} %vel.1, s32[3,128]{1,0:T(4,128)} %cen_in.1, s32[1]{0:T(128)S(6)} %copy.13.counts_in, s32[128,128]{1,0:T(8,128)} %points_in.1, ...), custom_call_target="tpu_custom_call" | custom-call | tf_op jit(solution)/shard_map/brick/pallas_call | solution.py:437
  31.1 1.8 %pass_on.1 = (f32[16,32,128]{2,1,0:T(8,128)}, f32[32,128]{1,0:T(8,128)}, f32[3,128,128]{2,1,0:T(8,128)}, f32[6,128]{1,0:T(8,128)}) custom-call(f32[16,32,128]{2,1,0:T(8,128)} %get-tuple-element.8.refs_0_, f32[32,128]{1,0:T(8,128)} %get-tuple-element.9.refs_1_, f32[3,128,128]{2,1,0:T(8,128)} %get-tuple-element.10.refs_2_, f32[6,128]{1,0:T(8,128)} %get-tuple-element.11.refs_3_), custom_call_target="tpu_custom_call" | custom-call | tf_op jit(solution)/shard_map/pass_on/pallas_call | solution.py:465

commit v3 on v2

--- a/solution.py
+++ b/solution.py
@@ -31,9 +31,9 @@
 
 
 def brick_kernel(
-    frac, vel, cen_in, counts_in, points_in, active_in, start_in, mass_in, inertia_in,
+    frac, vel, cen_in, counts, points_in, active_in, start_in, mass_in, inertia_in,
     fout, curv, mult, motion,
-    cen, counts, points, active, rigid, mass, inertia, ED, ER, EC, WT, A, AT, SM, CB, RM, T,
+    cen, points, active, rigid, mass, inertia, ED, ER, EC, WT, A, AT, SM, CB, RM, T,
     F, QU, QD, RQL, RQH, PL, PR, RL, RR, RZ, RZF, SQ, HB, HP, HX, HY, HC, HS, HN, HM,
     in_sem, send, recv, hsend, hrecv,
 ):
@@ -53,7 +53,7 @@
         pltpu.make_async_copy(src, dst, in_sem.at[4 + k])
         for k, (src, dst) in enumerate((
             (points_in, points), (active_in, active), (start_in, rigid), (mass_in, mass),
-            (inertia_in, inertia), (cen_in, cen), (counts_in, counts),
+            (inertia_in, inertia), (cen_in, cen),
         ))
     ]
     for c in small:
@@ -414,6 +414,10 @@
     curv[...] = top / (metric * jnp.sqrt(metric))
 
 
+def pinned(x):
+    return pltpu.with_memory_space_constraint(x, pltpu.HBM)
+
+
 def pass_kernel(*refs):
     n = (len(refs) - 1) // 2
     moves = [pltpu.make_async_copy(refs[k], refs[n + k], refs[-1].at[k]) for k in range(n)]
@@ -437,10 +441,10 @@
     results = pl.pallas_call(
         brick_kernel,
         out_shape=outs,
-        in_specs=[hbm] * 9,
+        in_specs=[hbm] * 3 + [pl.BlockSpec(memory_space=pltpu.SMEM)] + [hbm] * 5,
         out_specs=(vmem,) * 4,
         scratch_shapes=[
-            pltpu.SMEM((3, 128), I32), pltpu.SMEM((1,), I32),
+            pltpu.SMEM((3, 128), I32),
             room(128, 128, dtype=I32), room(128, 128, dtype=I32), room(6, 128), room(1, 128), room(1, 128),
             room(128, 128, dtype=I32), room(128, 128, dtype=I32), room(128, 128, dtype=I32),
             room(128, 128), room(128, 128), room(128, 128), room(3, 128, 128), room(24, 128, 128), room(128, 128),
@@ -450,24 +454,25 @@
             room(3, 4, 32, 128), room(4, 32, 128), room(18, 32, 128),
             room(32, 128), room(32, 128), room(2, 2, 8, 128), room(2, 2, 32, 128), room(2, 4, 8, 128),
             room(2, 48, 128), room(48, 128), room(48, 128),
-            pltpu.SemaphoreType.DMA((11,)),
+            pltpu.SemaphoreType.DMA((10,)),
             pltpu.SemaphoreType.DMA((18,)), pltpu.SemaphoreType.DMA((18,)),
             pltpu.SemaphoreType.DMA((17,)), pltpu.SemaphoreType.DMA((17,)),
         ],
         compiler_params=pltpu.CompilerParams(
-            collective_id=0, has_side_effects=True, vmem_limit_bytes=60 << 20
+            collective_id=0, has_side_effects=True, vmem_limit_bytes=40 << 20
         ),
         name="brick",
     )(
-        fraction, velocity, centres, counts, points, active_points, rigid_start,
-        mass.reshape(1, 128), inertia.reshape(1, 128),
+        *(pinned(x) for x in (fraction, velocity, centres)), counts,
+        *(pinned(x) for x in (points, active_points, rigid_start, mass.reshape(1, 128), inertia.reshape(1, 128))),
     )
     return pl.pallas_call(
         pass_kernel,
         out_shape=outs,
-        in_specs=[vmem] * 4,
+        in_specs=[anywhere] * 4,
         out_specs=(hbm,) * 4,
         scratch_shapes=[pltpu.SemaphoreType.DMA((4,))],
+        compiler_params=pltpu.CompilerParams(vmem_limit_bytes=4 << 20),
         name="pass_on",
     )(*results)
 

time: 33.1 us -> 31.3 us (0.946)
  Pallas kernels: 31.6 us -> 29.9 us
    pallas_call x2, Pallas kernels: 31.6 us -> 29.9 us  [the longest x1 29.1 us: body(): pl.pallas_call(brick_kernel, out_shape=outs, in_specs=[hbm] * 3 + [pl.Blo...]
where the time goes in v3:
time: 31.3 us; the launch traced here: 31.2 us
  Pallas kernels  29.9 us (96%)
  between operations  1.29 us (4%)
    pallas_call x1, Pallas kernels, body(): pl.pallas_call(brick_kernel, out_shape=outs, in_specs=[hbm] * 3 + [pl.Blo...  29.1 us
    pallas_call x1, Pallas kernels, body(): pl.pallas_call(pass_kernel, out_shape=outs, in_specs=[anywhere] * 4, out_...  0.81 us

profile of v3, /device:TPU:1, one launch (start us, length us, event | category | flops | bytes accessed | tf_op | source)
XLA Modules:
  0.0 31.2 jit_solution(17660432389367697332)
XLA Ops:
  1.3 29.1 %brick.1 = (f32[16,32,128]{2,1,0:T(8,128)S(1)}, f32[32,128]{1,0:T(8,128)S(1)}, f32[3,128,128]{2,1,0:T(8,128)S(1)}, f32[6,128]{1,0:T(8,128)S(1)}) custom-call(f32[16,32,128]{2,1,0:T(8,128)} %frac.1, f32[3,16,32,128]{3,2,1,0:T(8,128)} %vel.1, s32[3,128]{1,0:T(4,128)} %cen_in.1, s32[1]{0:T(128)S(6)} %copy.13.counts, s32[128,128]{1,0:T(8,128)} %points_in.1, ...), custom_call_target="tpu_custom_call" | custom-call | tf_op jit(solution)/shard_map/brick/pallas_call | solution.py:441
  30.4 0.8 %pass_on.1 = (f32[16,32,128]{2,1,0:T(8,128)}, f32[32,128]{1,0:T(8,128)}, f32[3,128,128]{2,1,0:T(8,128)}, f32[6,128]{1,0:T(8,128)}) custom-call(f32[16,32,128]{2,1,0:T(8,128)S(1)} %get-tuple-element.8.refs_0_, f32[32,128]{1,0:T(8,128)S(1)} %get-tuple-element.9.refs_1_, f32[3,128,128]{2,1,0:T(8,128)S(1)} %get-tuple-element.10.refs_2_, ...), custom_call_target="tpu_custom_call" | custom-call | tf_op jit(solution)/shard_map/pass_on/pallas_call | solution.py:469

commit v4 on v3

v4 whole, which is shorter than its diff:
```python
import jax
import jax.numpy as jnp
from jax import lax
from jax.experimental import pallas as pl
from jax.experimental.pallas import tpu as pltpu
from jax.sharding import PartitionSpec as P

MESH = pl.DeviceIdType.MESH
GROUP = 16
F32 = jnp.float32
I32 = jnp.int32

ACROSS = [(dx, dy) for dx in (-1, 0, 1) for dy in (-1, 0, 1) if dx or dy]


def lanes_of(shape):
    return lax.broadcasted_iota(I32, shape, len(shape) - 1)


def loop(steps, step, per=1):
    def some(g, _):
        for j in range(per):
            step(g * per + j, 0)
        return 0

    if steps == per:
        for k in range(steps):
            step(k, 0)
    else:
        lax.fori_loop(0, steps // per, some, 0)


def rows8(first):
    return pl.ds(first if isinstance(first, int) else pl.multiple_of(first, 8), 8)


def turn(x, by):
    by %= 128
    return pltpu.roll(x, by, x.ndim - 1) if by else x


def along(x, idx, axis):
    return jnp.take_along_axis(x, idx, axis=axis, mode="promise_in_bounds")


def cross(a, b):
    return [a[1] * b[2] - a[2] * b[1], a[2] * b[0] - a[0] * b[2], a[0] * b[1] - a[1] * b[0]]


def brick_kernel(
    frac, vel, cen_in, counts, points_in, active_in, start_in, mass_in, inertia_in,
    fout, curv, mult, motion,
    cen, points, active, rigid, mass, inertia, ED, ER, EC, WT, A, AT, SM, CB, RM, T,
    F, QU, QD, RQL, RQH, RV, PL, PR, RL, RR, PH, PV, SH, SQ, HB, HP, HY, HS, HN, HM,
    in_sem, send, recv, hsend, hrecv,
):
    gx, gy, gz = (lax.axis_index(a) for a in ("gx", "gy", "gz"))

    def place(dx, dy, dz):
        return (lax.rem(gx + dx + 16, 16), lax.rem(gy + dy + 8, 8), gz if dz == 0 else 1 - gz)

    everyone = [(dx, dy, dz) for dz in (0, 1) for dx, dy in ACROSS] + [(0, 0, 1)]
    own = [
        pltpu.make_async_copy(vel, T.at[0, :, 4:20, 8:40, :], in_sem.at[0]),
        pltpu.make_async_copy(frac, F.at[4:20, 8:40, :], in_sem.at[1]),
    ]
    for c in own:
        c.start()
    small = [
        pltpu.make_async_copy(src, dst, in_sem.at[2 + k])
        for k, (src, dst) in enumerate((
            (points_in, points), (active_in, active), (start_in, rigid), (mass_in, mass),
            (inertia_in, inertia), (cen_in, cen),
        ))
    ]
    for c in small:
        c.start()

    barrier = pltpu.get_barrier_semaphore()
    for off in everyone:
        pl.semaphore_signal(barrier, inc=1, device_id=place(*off), device_id_type=MESH)

    low = 12 * (1 - gz)
    copies = {}
    count = [0]

    def start(key, src, dst, off):
        k = count[0]
        count[0] += 1
        c = pltpu.make_async_remote_copy(
            src_ref=src, dst_ref=dst, send_sem=send.at[k], recv_sem=recv.at[k], device_id=place(*off),
            device_id_type=MESH,
        )
        c.start()
        copies[key] = c

    for c in own:
        c.wait()

    def layers(c, d):
        return T.at[0, c, d] if c < 3 else F.at[d]

    def pack_rows(g, _):
        for dd in range(4):
            for c in range(4):
                at = 12 * dd + 3 * c
                QU[g, at : at + 3, :] = layers(c, 4 + 4 * g + dd)[37:40, :]
                QD[g, at : at + 3, :] = layers(c, 4 + 4 * g + dd)[8:11, :]
        return 0

    loop(4, pack_rows, 1)
    pl.semaphore_wait(barrier, len(everyone))
    for dx, src, dst in ((1, QU, RQL), (-1, QD, RQH)):
        start((dx, 0, 0), src, dst.at[1:5], (dx, 0, 0))
        start((dx, 0, 1), src.at[3 * (1 - gz)], dst.at[5 * gz], (dx, 0, 1))

    start("z", vel.at[:, pl.ds(low, 4)], T.at[0, :, pl.ds(20 * gz, 4), 8:40, :], (0, 0, 1))
    start("zf", frac.at[pl.ds(low, 4)], F.at[pl.ds(20 * gz, 4), 8:40, :], (0, 0, 1))

    lane = lanes_of((8, 128))
    spot = lane // 8
    first = (lane % 8) < 4

    def pack_lanes(t, _):
        rows = rows8(8 + 8 * t)
        both = []
        for c in range(4):
            acc = None
            for d in range(16):
                v = turn(layers(c, 4 + d)[rows, :], 8 * d + 4)
                acc = v if d == 0 else jnp.where(spot == d, v, acc)
            both.append(acc)
        for h in range(2):
            a, b = both[2 * h], both[2 * h + 1]
            PL[h, t] = jnp.where(first, a, turn(b, 4))
            PR[h, t] = jnp.where(first, turn(a, -4), b)
        return 0

    loop(4, pack_lanes, 4)
    for dx in (0, 1, -1):
        ts, td = {0: (slice(0, 4), slice(1, 5)), 1: (3, 0), -1: (0, 5)}[dx]
        for dz in (0, 1):
            for dy, src, dst in ((1, PL, RL), (-1, PR, RR)):
                start((dx, dy, dz), src.at[:, ts], dst.at[2 * gz if dz else 1, :, td], (dx, dy, dz))

    RQL[5 * gz] = jnp.zeros((48, 128), F32)
    RQH[5 * gz] = jnp.zeros((48, 128), F32)
    RL[2 * gz] = jnp.zeros((2, 6, 8, 128), F32)
    RR[2 * gz] = jnp.zeros((2, 6, 8, 128), F32)
    blank = jnp.zeros((4, 32, 128), F32)
    for c in range(3):
        T[0, c, pl.ds(20 * gz, 4), 8:40, :] = blank
        T[1, c, pl.ds(20 * gz, 4), 8:40, :] = blank
    F[pl.ds(20 * gz, 4), 8:40, :] = blank

    def aside(x):
        return jnp.where(lanes_of(x.shape) < 64, turn(x, 60), turn(x, 68))

    def fill_aside(k, _):
        for c in range(3):
            T[1, c, 4 + k, 8:40, :] = aside(T[0, c, 4 + k, 8:40, :])
        return 0

    loop(16, fill_aside, 4)

    for c in small:
        c.wait()
    A[...] = jnp.zeros((128, 128), F32)
    A[0:6, :] = rigid[...]
    A[6:7, :] = mass[...]
    A[7:8, :] = inertia[...]
    AT[...] = A[...].T
    owned = counts[0]
    ones = jnp.ones((256, 128), jnp.bfloat16)

    def total(x):
        return jnp.dot(x.astype(jnp.bfloat16), ones[:128], preferred_element_type=F32)

    def prepare(k, _):
        base = pl.multiple_of(32 * k, 32)
        rows = pl.ds(base, 32)
        code = points[rows, :]
        ed = (code * 1338) >> 16
        rest = code - ed * 49
        er = (rest * 9363) >> 16
        ec = rest - er * 7
        ED[rows, :] = ed
        ER[rows, :] = er
        EC[rows, :] = ec
        alive = ((lax.broadcasted_iota(I32, (32, 128), 0) + base) < owned).astype(F32)
        w = active[rows, :].astype(F32) * alive
        WT[rows, :] = w
        e = [(x - 3).astype(F32) for x in (ed, er, ec)]
        we = [w * x for x in e]
        m0 = total(w)
        m1 = [total(x) for x in we]
        m2 = {(i, j): total(we[i] * e[j]) for i in range(3) for j in range(i, 3)}
        J = [m2[(1, 1)] + m2[(2, 2)], m2[(0, 0)] + m2[(2, 2)], m2[(0, 0)] + m2[(1, 1)]]
        columns = AT[rows, :]
        column = [jnp.broadcast_to(columns[:, c : c + 1], (32, 128)) for c in range(8)]
        for c, x in enumerate(column + [m0] + m1 + J + [m2[(0, 1)], m2[(0, 2)], m2[(1, 2)]]):
            CB[c, rows, :] = x
        force, torque = pull(column[0:3], column[3:6], m0, m1, J, m2[(0, 1)], m2[(0, 2)], m2[(1, 2)])
        for c, x in enumerate(force + torque):
            CB[18 + c, rows, :] = x
        return 0

    def pull(linear, angular, m0, m1, J, xy, xz, yz):
        turned = cross(angular, m1)
        force = [m0 * linear[c] + turned[c] for c in range(3)]
        lever = cross(m1, linear)
        torque = [
            lever[0] + (J[0] * angular[0] - xy * angular[1] - xz * angular[2]),
            lever[1] + (J[1] * angular[1] - xy * angular[0] - yz * angular[2]),
            lever[2] + (J[2] * angular[2] - xz * angular[0] - yz * angular[1]),
        ]
        return force, torque

    loop(4, prepare, 2)
    copies["z"].wait()
    copies["zf"].wait()

    def fill_aside_partner(k, _):
        for c in range(3):
            T[1, c, 20 * (1 - gz) + k, 8:40, :] = aside(T[0, c, 20 * (1 - gz) + k, 8:40, :])
        return 0

    loop(4, fill_aside_partner, 4)

    in_low, in_high = (gx > 0).astype(F32), (gx < 15).astype(F32)
    in_left, in_right = (gy > 0).astype(F32), (gy < 7).astype(F32)
    ranks = ((1, RQL, 5, in_low), (-1, RQH, 40, in_high))
    for dx, src, to, here in ranks:
        copies[(dx, 0, 0)].wait()
        copies[(dx, 0, 1)].wait()

        def unpack_rows(g, _):
            for dd in range(4):
                for c in range(4):
                    at = 12 * dd + 3 * c
                    layers(c, 4 * g + dd)[to : to + 3, :] = src[g, at : at + 3, :] * here
            return 0

        loop(6, unpack_rows, 2)

    for dy in (1, -1):
        for dx in (0, 1, -1):
            copies[(dx, dy, 0)].wait()
            copies[(dx, dy, 1)].wait()

    def merge(t, _):
        rows = rows8(8 * t)
        here = jnp.where(t == 0, in_low, jnp.where(t == 5, in_high, 1.0))
        left, right = in_left * here, in_right * here
        for lev in range(3):
            for c in range(4):
                a, b = RL[lev, c // 2, t] * left, RR[lev, c // 2, t] * right
                if c > 0:
                    PH[c - 1, lev, rows, :] = (
                        jnp.where(first, turn(a, -4), b) if c % 2 else jnp.where(first, a, turn(b, 4))
                    )
                if c < 3:
                    PV[c, lev, rows, :] = (
                        jnp.where(first, turn(b, -4), a) if c % 2 else jnp.where(first, b, turn(a, 4))
                    )
        return 0

    loop(6, merge, 3)

    wide = lanes_of((40, 128))
    head, tail = wide == 0, wide == 127

    def flux_of(speed, below, above):
        return jnp.maximum(speed, 0.0) * below + jnp.minimum(speed, 0.0) * above

    def swept(q, flux_low, flux_high, speed_low, speed_high):
        return q - (flux_high - flux_low) + q * (speed_high - speed_low)

    def sweep_of(q, u):
        lo, hi = 0.5 * (u[0] + u[1]), 0.5 * (u[1] + u[2])
        return swept(q[1], flux_of(lo, q[0], q[1]), flux_of(hi, q[1], q[2]), lo, hi)

    for lev in range(3):
        SH[lev] = sweep_of(
            [PH[2, lev, 6 + o : 46 + o, :] for o in range(3)], [PH[0, lev, 6 + o : 46 + o, :] for o in range(3)]
        )

    def sweep_xy(k, _):
        d = 3 + k
        q = sweep_of(
            [F[d, 6 + o : 46 + o, :] for o in range(3)], [T[0, 1, d, 6 + o : 46 + o, :] for o in range(3)]
        )
        u = T[0, 2, d, 7:47, :]
        lev = jnp.where(k == 0, 0, jnp.where(k == 17, 2, 1))
        by = 124 - 8 * ((k + 15) % 16)
        qh, uh = pltpu.roll(SH[lev], by, 1), pltpu.roll(PH[1, lev, 7:47, :], by, 1)
        ql, ul = turn(jnp.where(tail, qh, q), 1), turn(jnp.where(tail, uh, u), 1)
        qr, ur = turn(jnp.where(head, qh, q), -1), turn(jnp.where(head, uh, u), -1)
        SQ[k] = sweep_of([ql, q, qr], [ul, u, ur])
        return 0

    loop(18, sweep_xy, 6)

    def sweep_z(k, carry):
        total_height, q, u, speed, flux = carry
        above, u_above = SQ[k + 2], T[0, 0, 5 + k, 7:47, :]
        speed_above = 0.5 * (u + u_above)
        flux_above = flux_of(speed_above, q, above)
        new = swept(q, flux, flux_above, speed, speed_above)
        fout[k, 7:47, :] = new
        return total_height + new, above, u_above, speed_above, flux_above

    u0, u1 = T[0, 0, 3, 7:47, :], T[0, 0, 4, 7:47, :]
    speed0 = 0.5 * (u0 + u1)
    HB[...] = lax.fori_loop(
        0, 16, sweep_z, (jnp.zeros((40, 128), F32), SQ[1], u1, speed0, flux_of(speed0, SQ[0], SQ[1]))
    )[0]

    heights = []
    for j, (dy, dz) in enumerate([(1, 1), (-1, 1), (1, 0), (-1, 0), (0, 1)]):
        c = pltpu.make_async_remote_copy(
            src_ref=HB, dst_ref=HY.at[dz, (dy < 0) * 1] if dy else HP, send_sem=hsend.at[j], recv_sem=hrecv.at[j],
            device_id=place(0, dy, dz), device_id_type=MESH,
        )
        c.start()
        heights.append(c)

    for dx, src, to, here in ranks:
        def shift_rows(g, _):
            RV[g] = aside(src[g] * here)
            return 0

        def place_rows(g, _):
            for dd in range(4):
                for c in range(3):
                    at = 12 * dd + 3 * c
                    T[1, c, 4 * g + dd, to : to + 3, :] = RV[g, at : at + 3, :]
            return 0

        loop(6, shift_rows, 3)
        loop(6, place_rows, 2)
    joint = (lane >= 60) & (lane < 68)

    def unpack_lanes(t, _):
        rows = rows8(8 * t)
        for c in range(3):
            for lev, near in ((0, range(13, 16)), (1, range(16)), (2, range(3))):
                v = PV[c, lev, rows, :]
                for d in near:
                    at = 4 + 16 * (lev - 1) + d
                    pltpu.store(T.at[1, c, at, rows, :], turn(v, 60 - 8 * d), mask=joint)
        return 0

    loop(6, unpack_lanes, 1)

    row8 = lax.broadcasted_iota(I32, (8, 128), 0)

    def sample(g, _):
        base = pl.multiple_of(g * GROUP, GROUP)
        tiles = [[None] * (GROUP // 8) for _ in range(3)]
        for s in range(GROUP):
            q = base + s
            d0 = jnp.clip(cen[0, q] - 2, 1, 16)
            r0 = jnp.clip(cen[1, q] + 2, 5, 36)
            jc = cen[2, q] - 3
            at_left, at_right = (jc < 3).astype(I32), (jc > 124).astype(I32)
            side = at_left + at_right
            first_lane = jc - 3 + 68 * (at_left - at_right)
            e_d = jnp.broadcast_to(ED[pl.ds(q, 1), :], (8, 128))
            e_r = jnp.broadcast_to(ER[pl.ds(q, 1), :], (8, 128))
            idx = (jnp.broadcast_to(EC[pl.ds(q, 1), :], (8, 128)) + first_lane) & 127
            picks = [e_d == k for k in range(1, 7)]
            for c in range(3):
                acc = None
                for k in range(7):
                    v = along(T[side, c, d0 + k, pl.ds(r0, 8), :], idx, 1)
                    acc = v if k == 0 else jnp.where(picks[k - 1], v, acc)
                res = along(acc, e_r, 0)
                old = tiles[c][s // 8]
                tiles[c][s // 8] = res if s % 8 == 0 else jnp.where(row8 == s % 8, res, old)
        for c in range(3):
            SM[c, pl.ds(base, GROUP), :] = jnp.concatenate(tiles[c], axis=0)
        return 0

    loop(128 // GROUP, sample, 1)

    def total_of(x):
        high = x.astype(jnp.bfloat16)
        rest = (x - high.astype(F32)).astype(jnp.bfloat16)
        return jnp.dot(jnp.concatenate([high, rest], axis=1), ones, preferred_element_type=F32)

    def iterate(k, _):
        rows = pl.ds(pl.multiple_of(32 * k, 32), 32)
        s = [SM[c, rows, :] for c in range(3)]
        w = WT[rows, :]
        e = [(x[rows, :] - 3).astype(F32) for x in (ED, ER, EC)]
        ws = [w * x for x in s]
        S = [total_of(x) for x in ws]
        Q = [total_of(x) for x in cross(e, ws)]
        n = [CB[c, rows, :] for c in range(24)]
        linear, angular, force, torque = n[0:3], n[3:6], n[18:21], n[21:24]
        linear1 = [linear[c] + n[6] * (S[c] - force[c]) for c in range(3)]
        angular1 = [angular[c] + n[7] * (Q[c] - torque[c]) for c in range(3)]
        force1, torque1 = pull(linear1, angular1, n[8], n[9:12], n[12:15], n[15], n[16], n[17])
        last = [linear[c] + n[6] * (1.5 * S[c] - 0.5 * force[c] - force1[c]) for c in range(3)]
        last += [angular[c] + n[7] * (1.5 * Q[c] - 0.5 * torque[c] - torque1[c]) for c in range(3)]
        both = [0.5 * linear[c] + linear1[c] for c in range(3)]
        spin = cross([0.5 * angular[c] + angular1[c] for c in range(3)], e)
        for c in range(3):
            mult[c, rows, :] = 1.5 * ws[c] - w * (both[c] + spin[c])
        lanes = lanes_of((32, 128))
        out = jnp.zeros((32, 128), F32)
        for c in range(6):
            out = jnp.where(lanes == c, last[c], out)
        alive = ((lax.broadcasted_iota(I32, (32, 128), 0) + 32 * k) < owned).astype(F32)
        RM[rows, :] = out * alive
        return 0

    loop(4, iterate, 2)
    motion[...] = RM[...].T[0:6, :]

    for c in heights:
        c.wait()

    row = lax.broadcasted_iota(I32, (40, 128), 0)
    inside = jnp.where(row == 0, in_low, jnp.where(row == 33, in_high, 1.0))
    h = (HB[...] + HP[...]) * inside
    hh = jnp.where(wide >= 64, (HY[0, 0] + HY[1, 0]) * in_left, (HY[0, 1] + HY[1, 1]) * in_right) * inside
    HS[...] = h
    HN[...] = turn(jnp.where(head, hh, h), -1)
    HM[...] = turn(jnp.where(tail, hh, h), 1)
    middle, east, west = HS[1:33], HS[2:34], HS[0:32]
    north, south = HN[1:33], HM[1:33]
    slope_x, slope_y = 0.5 * (east - west), 0.5 * (north - south)
    bend_xx = east - 2.0 * middle + west
    bend_yy = north - 2.0 * middle + south
    bend_xy = 0.25 * (HN[2:34] - HM[2:34] - HN[0:32] + HM[0:32])
    metric = 1.0 + slope_x * slope_x + slope_y * slope_y
    top = (
        bend_xx * (1.0 + slope_y * slope_y) + bend_yy * (1.0 + slope_x * slope_x)
        - 2.0 * slope_x * slope_y * bend_xy
    )
    curv[...] = top / (metric * jnp.sqrt(metric))


def pinned(x):
    return pltpu.with_memory_space_constraint(x, pltpu.HBM)


def pass_kernel(*refs):
    n = (len(refs) - 1) // 2
    sources = [refs[0].at[:, 8:40, :]] + list(refs[1:n])
    moves = [pltpu.make_async_copy(sources[k], refs[n + k], refs[-1].at[k]) for k in range(n)]
    for c in moves:
        c.start()
    for c in moves:
        c.wait()


def body(fraction, velocity, centres, points, active_points, counts, rigid_start, mass, inertia):
    vmem, anywhere = pl.BlockSpec(memory_space=pltpu.VMEM), pl.BlockSpec(memory_space=pl.ANY)
    hbm = pl.BlockSpec(memory_space=pltpu.HBM)

    def f32(*shape):
        return jax.ShapeDtypeStruct(shape, F32)

    def room(*shape, dtype=F32):
        return pltpu.VMEM(shape, dtype)

    outs = (f32(16, 32, 128), f32(32, 128), f32(3, 128, 128), f32(6, 128))
    results = pl.pallas_call(
        brick_kernel,
        out_shape=(f32(16, 48, 128),) + outs[1:],
        in_specs=[hbm] * 3 + [pl.BlockSpec(memory_space=pltpu.SMEM)] + [hbm] * 5,
        out_specs=(vmem,) * 4,
        scratch_shapes=[
            pltpu.SMEM((3, 128), I32),
            room(128, 128, dtype=I32), room(128, 128, dtype=I32), room(6, 128), room(1, 128), room(1, 128),
            room(128, 128, dtype=I32), room(128, 128, dtype=I32), room(128, 128, dtype=I32),
            room(128, 128), room(128, 128), room(128, 128), room(3, 128, 128), room(24, 128, 128), room(128, 128),
            room(2, 3, 24, 48, 128), room(24, 48, 128),
            room(4, 48, 128), room(4, 48, 128), room(6, 48, 128), room(6, 48, 128), room(6, 48, 128),
            room(2, 4, 8, 128), room(2, 4, 8, 128), room(3, 2, 6, 8, 128), room(3, 2, 6, 8, 128),
            room(3, 3, 48, 128), room(3, 3, 48, 128), room(3, 40, 128), room(18, 40, 128),
            room(40, 128), room(40, 128), room(2, 2, 40, 128), room(40, 128), room(40, 128), room(40, 128),
            pltpu.SemaphoreType.DMA((8,)),
            pltpu.SemaphoreType.DMA((18,)), pltpu.SemaphoreType.DMA((18,)),
            pltpu.SemaphoreType.DMA((5,)), pltpu.SemaphoreType.DMA((5,)),
        ],
        compiler_params=pltpu.CompilerParams(
            collective_id=0, has_side_effects=True, vmem_limit_bytes=40 << 20
        ),
        name="brick",
    )(
        *(pinned(x) for x in (fraction, velocity, centres)), counts,
        *(pinned(x) for x in (points, active_points, rigid_start, mass.reshape(1, 128), inertia.reshape(1, 128))),
    )
    return pl.pallas_call(
        pass_kernel,
        out_shape=outs,
        in_specs=[anywhere] * 4,
        out_specs=(hbm,) * 4,
        scratch_shapes=[pltpu.SemaphoreType.DMA((4,))],
        compiler_params=pltpu.CompilerParams(vmem_limit_bytes=4 << 20),
        name="pass_on",
    )(*results)


def solution(mesh):
    bricks = ("gx", "gy", "gz")
    placed = (
        P("gz", "gx", "gy"), P(None, "gz", "gx", "gy"), P(None, bricks), P(bricks, None), P(bricks, None),
        P(bricks), P(None, bricks), P(bricks), P(bricks),
    )
    return jax.shard_map(
        body, mesh=mesh, in_specs=placed,
        out_specs=(P("gz", "gx", "gy"), P("gx", "gy"), P(None, bricks, None), P(None, bricks)),
        check_vma=False,
    )
```

time: 31.3 us -> 27.1 us (0.87)
  Pallas kernels: 29.9 us -> 25.7 us
    pallas_call x1, Pallas kernels: 29.1 us -> 24.9 us  [body(): pl.pallas_call(brick_kernel, out_shape=(f32(16, 48, 128),) + outs[1:], in...]
where the time goes in v4:
time: 27.1 us; the launch traced here: 27 us
  Pallas kernels  25.7 us (95%)
  between operations  1.29 us (5%)
    pallas_call x1, Pallas kernels, body(): pl.pallas_call(brick_kernel, out_shape=(f32(16, 48, 128),) + outs[1:], in...  24.9 us
    pallas_call x1, Pallas kernels, body(): pl.pallas_call(pass_kernel, out_shape=outs, in_specs=[anywhere] * 4, out_...  0.81 us

profile of v4, /device:TPU:1, one launch (start us, length us, event | category | flops | bytes accessed | tf_op | source)
XLA Modules:
  0.0 27.0 jit_solution(14576047731639153545)
XLA Ops:
  1.3 24.9 %brick.1 = (f32[16,48,128]{2,1,0:T(8,128)S(1)}, f32[32,128]{1,0:T(8,128)S(1)}, f32[3,128,128]{2,1,0:T(8,128)S(1)}, f32[6,128]{1,0:T(8,128)S(1)}) custom-call(f32[16,32,128]{2,1,0:T(8,128)} %frac.1, f32[3,16,32,128]{3,2,1,0:T(8,128)} %vel.1, s32[3,128]{1,0:T(4,128)} %cen_in.1, s32[1]{0:T(128)S(6)} %copy.13.counts, s32[128,128]{1,0:T(8,128)} %points_in.1, ...), custom_call_target="tpu_custom_call" | custom-call | tf_op jit(solution)/shard_map/brick/pallas_call | solution.py:471
  26.2 0.8 %pass_on.1 = (f32[16,32,128]{2,1,0:T(8,128)}, f32[32,128]{1,0:T(8,128)}, f32[3,128,128]{2,1,0:T(8,128)}, f32[6,128]{1,0:T(8,128)}) custom-call(f32[16,48,128]{2,1,0:T(8,128)S(1)} %get-tuple-element.8.refs_0_, f32[32,128]{1,0:T(8,128)S(1)} %get-tuple-element.9.refs_1_, f32[3,128,128]{2,1,0:T(8,128)S(1)} %get-tuple-element.10.refs_2_, ...), custom_call_target="tpu_custom_call" | custom-call | tf_op jit(solution)/shard_map/pass_on/pallas_call | solution.py:498

commit v5 on v4

--- a/solution.py
+++ b/solution.py
@@ -6,7 +6,7 @@
 from jax.sharding import PartitionSpec as P
 
 MESH = pl.DeviceIdType.MESH
-GROUP = 16
+GROUP = 64
 F32 = jnp.float32
 I32 = jnp.int32
 
@@ -66,6 +66,10 @@
     ]
     for c in own:
         c.start()
+    barrier = pltpu.get_barrier_semaphore()
+    for off in everyone:
+        pl.semaphore_signal(barrier, inc=1, device_id=place(*off), device_id_type=MESH)
+
     small = [
         pltpu.make_async_copy(src, dst, in_sem.at[2 + k])
         for k, (src, dst) in enumerate((
@@ -75,10 +79,6 @@
     ]
     for c in small:
         c.start()
-
-    barrier = pltpu.get_barrier_semaphore()
-    for off in everyone:
-        pl.semaphore_signal(barrier, inc=1, device_id=place(*off), device_id_type=MESH)
 
     low = 12 * (1 - gz)
     copies = {}
@@ -243,6 +243,21 @@
 
         loop(6, unpack_rows, 2)
 
+    for dx, src, to, here in ranks:
+        def shift_rows(g, _):
+            RV[g] = aside(src[g] * here)
+            return 0
+
+        def place_rows(g, _):
+            for dd in range(4):
+                for c in range(3):
+                    at = 12 * dd + 3 * c
+                    T[1, c, 4 * g + dd, to : to + 3, :] = RV[g, at : at + 3, :]
+            return 0
+
+        loop(6, shift_rows, 3)
+        loop(6, place_rows, 2)
+
     for dy in (1, -1):
         for dx in (0, 1, -1):
             copies[(dx, dy, 0)].wait()
@@ -325,20 +340,6 @@
         c.start()
         heights.append(c)
 
-    for dx, src, to, here in ranks:
-        def shift_rows(g, _):
-            RV[g] = aside(src[g] * here)
-            return 0
-
-        def place_rows(g, _):
-            for dd in range(4):
-                for c in range(3):
-                    at = 12 * dd + 3 * c
-                    T[1, c, 4 * g + dd, to : to + 3, :] = RV[g, at : at + 3, :]
-            return 0
-
-        loop(6, shift_rows, 3)
-        loop(6, place_rows, 2)
     joint = (lane >= 60) & (lane < 68)
 
     def unpack_lanes(t, _):
@@ -351,7 +352,7 @@
                     pltpu.store(T.at[1, c, at, rows, :], turn(v, 60 - 8 * d), mask=joint)
         return 0
 
-    loop(6, unpack_lanes, 1)
+    loop(6, unpack_lanes, 3)
 
     row8 = lax.broadcasted_iota(I32, (8, 128), 0)
 
@@ -416,7 +417,7 @@
         RM[rows, :] = out * alive
         return 0
 
-    loop(4, iterate, 2)
+    loop(4, iterate, 4)
     motion[...] = RM[...].T[0:6, :]
 
     for c in heights:

time: 27.1 us -> 26.2 us (0.967)
  Pallas kernels: 25.7 us -> 24.8 us
    pallas_call x1, Pallas kernels: 24.9 us -> 24 us  [body(): pl.pallas_call(brick_kernel, out_shape=(f32(16, 48, 128),) + outs[1:], in...]
where the time goes in v5:
time: 26.2 us; the launch traced here: 26.1 us
  Pallas kernels  24.8 us (95%)
  between operations  1.29 us (5%)
    pallas_call x1, Pallas kernels, body(): pl.pallas_call(brick_kernel, out_shape=(f32(16, 48, 128),) + outs[1:], in...  24 us
    pallas_call x1, Pallas kernels, body(): pl.pallas_call(pass_kernel, out_shape=outs, in_specs=[anywhere] * 4, out_...  0.81 us

profile of v5, /device:TPU:1, one launch (start us, length us, event | category | flops | bytes accessed | tf_op | source)
XLA Modules:
  0.0 26.1 jit_solution(4292557543355460130)
XLA Ops:
  1.3 24.0 %brick.1 = (f32[16,48,128]{2,1,0:T(8,128)S(1)}, f32[32,128]{1,0:T(8,128)S(1)}, f32[3,128,128]{2,1,0:T(8,128)S(1)}, f32[6,128]{1,0:T(8,128)S(1)}) custom-call(f32[16,32,128]{2,1,0:T(8,128)} %frac.1, f32[3,16,32,128]{3,2,1,0:T(8,128)} %vel.1, s32[3,128]{1,0:T(4,128)} %cen_in.1, s32[1]{0:T(128)S(6)} %copy.13.counts, s32[128,128]{1,0:T(8,128)} %points_in.1, ...), custom_call_target="tpu_custom_call" | custom-call | tf_op jit(solution)/shard_map/brick/pallas_call | solution.py:472
  25.3 0.8 %pass_on.1 = (f32[16,32,128]{2,1,0:T(8,128)}, f32[32,128]{1,0:T(8,128)}, f32[3,128,128]{2,1,0:T(8,128)}, f32[6,128]{1,0:T(8,128)}) custom-call(f32[16,48,128]{2,1,0:T(8,128)S(1)} %get-tuple-element.8.refs_0_, f32[32,128]{1,0:T(8,128)S(1)} %get-tuple-element.9.refs_1_, f32[3,128,128]{2,1,0:T(8,128)S(1)} %get-tuple-element.10.refs_2_, ...), custom_call_target="tpu_custom_call" | custom-call | tf_op jit(solution)/shard_map/pass_on/pallas_call | solution.py:499

commit v6 on v5

--- a/solution.py
+++ b/solution.py
@@ -108,7 +108,7 @@
                 QD[g, at : at + 3, :] = layers(c, 4 + 4 * g + dd)[8:11, :]
         return 0
 
-    loop(4, pack_rows, 1)
+    loop(4, pack_rows, 2)
     pl.semaphore_wait(barrier, len(everyone))
     for dx, src, dst in ((1, QU, RQL), (-1, QD, RQH)):
         start((dx, 0, 0), src, dst.at[1:5], (dx, 0, 0))
@@ -255,7 +255,7 @@
                     T[1, c, 4 * g + dd, to : to + 3, :] = RV[g, at : at + 3, :]
             return 0
 
-        loop(6, shift_rows, 3)
+        loop(6, shift_rows, 6)
         loop(6, place_rows, 2)
 
     for dy in (1, -1):
@@ -280,7 +280,7 @@
                     )
         return 0
 
-    loop(6, merge, 3)
+    loop(6, merge, 6)
 
     wide = lanes_of((40, 128))
     head, tail = wide == 0, wide == 127
@@ -327,8 +327,13 @@
 
     u0, u1 = T[0, 0, 3, 7:47, :], T[0, 0, 4, 7:47, :]
     speed0 = 0.5 * (u0 + u1)
+    def sweep_z_some(g, carry):
+        for j in range(4):
+            carry = sweep_z(g * 4 + j, carry)
+        return carry
+
     HB[...] = lax.fori_loop(
-        0, 16, sweep_z, (jnp.zeros((40, 128), F32), SQ[1], u1, speed0, flux_of(speed0, SQ[0], SQ[1]))
+        0, 4, sweep_z_some, (jnp.zeros((40, 128), F32), SQ[1], u1, speed0, flux_of(speed0, SQ[0], SQ[1]))
     )[0]
 
     heights = []
@@ -352,7 +357,7 @@
                     pltpu.store(T.at[1, c, at, rows, :], turn(v, 60 - 8 * d), mask=joint)
         return 0
 
-    loop(6, unpack_lanes, 3)
+    loop(6, unpack_lanes, 6)
 
     row8 = lax.broadcasted_iota(I32, (8, 128), 0)
 

time: 26.2 us -> 25.8 us (0.985)
  Pallas kernels: 24.8 us -> 24.4 us
    pallas_call x1, Pallas kernels: 24 us -> 23.6 us  [body(): pl.pallas_call(brick_kernel, out_shape=(f32(16, 48, 128),) + outs[1:], in...]
where the time goes in v6:
time: 25.8 us; the launch traced here: 25.7 us
  Pallas kernels  24.4 us (95%)
  between operations  1.29 us (5%)
    pallas_call x1, Pallas kernels, body(): pl.pallas_call(brick_kernel, out_shape=(f32(16, 48, 128),) + outs[1:], in...  23.6 us
    pallas_call x1, Pallas kernels, body(): pl.pallas_call(pass_kernel, out_shape=outs, in_specs=[anywhere] * 4, out_...  0.81 us

profile of v6, /device:TPU:1, one launch (start us, length us, event | category | flops | bytes accessed | tf_op | source)
XLA Modules:
  0.0 25.7 jit_solution(3168342587505443467)
XLA Ops:
  1.3 23.6 %brick.1 = (f32[16,48,128]{2,1,0:T(8,128)S(1)}, f32[32,128]{1,0:T(8,128)S(1)}, f32[3,128,128]{2,1,0:T(8,128)S(1)}, f32[6,128]{1,0:T(8,128)S(1)}) custom-call(f32[16,32,128]{2,1,0:T(8,128)} %frac.1, f32[3,16,32,128]{3,2,1,0:T(8,128)} %vel.1, s32[3,128]{1,0:T(4,128)} %cen_in.1, s32[1]{0:T(128)S(6)} %copy.13.counts, s32[128,128]{1,0:T(8,128)} %points_in.1, ...), custom_call_target="tpu_custom_call" | custom-call | tf_op jit(solution)/shard_map/brick/pallas_call | solution.py:477
  24.8 0.8 %pass_on.1 = (f32[16,32,128]{2,1,0:T(8,128)}, f32[32,128]{1,0:T(8,128)}, f32[3,128,128]{2,1,0:T(8,128)}, f32[6,128]{1,0:T(8,128)}) custom-call(f32[16,48,128]{2,1,0:T(8,128)S(1)} %get-tuple-element.8.refs_0_, f32[32,128]{1,0:T(8,128)S(1)} %get-tuple-element.9.refs_1_, f32[3,128,128]{2,1,0:T(8,128)S(1)} %get-tuple-element.10.refs_2_, ...), custom_call_target="tpu_custom_call" | custom-call | tf_op jit(solution)/shard_map/pass_on/pallas_call | solution.py:504

commit v7 on v6

--- a/solution.py
+++ b/solution.py
@@ -6,7 +6,7 @@
 from jax.sharding import PartitionSpec as P
 
 MESH = pl.DeviceIdType.MESH
-GROUP = 64
+GROUP = 128
 F32 = jnp.float32
 I32 = jnp.int32
 

time: 25.8 us -> 25.8 us (level)
  no operation moved by 1% of the time
where the time goes in v7:
time: 25.8 us; the launch traced here: 25.6 us
  Pallas kernels  24.4 us (95%)
  between operations  1.29 us (5%)
    pallas_call x1, Pallas kernels, body(): pl.pallas_call(brick_kernel, out_shape=(f32(16, 48, 128),) + outs[1:], in...  23.5 us
    pallas_call x1, Pallas kernels, body(): pl.pallas_call(pass_kernel, out_shape=outs, in_specs=[anywhere] * 4, out_...  0.81 us

profile of v7, /device:TPU:1, one launch (start us, length us, event | category | flops | bytes accessed | tf_op | source)
XLA Modules:
  0.0 25.6 jit_solution(2473017013803577433)
XLA Ops:
  1.3 23.5 %brick.1 = (f32[16,48,128]{2,1,0:T(8,128)S(1)}, f32[32,128]{1,0:T(8,128)S(1)}, f32[3,128,128]{2,1,0:T(8,128)S(1)}, f32[6,128]{1,0:T(8,128)S(1)}) custom-call(f32[16,32,128]{2,1,0:T(8,128)} %frac.1, f32[3,16,32,128]{3,2,1,0:T(8,128)} %vel.1, s32[3,128]{1,0:T(4,128)} %cen_in.1, s32[1]{0:T(128)S(6)} %copy.13.counts, s32[128,128]{1,0:T(8,128)} %points_in.1, ...), custom_call_target="tpu_custom_call" | custom-call | tf_op jit(solution)/shard_map/brick/pallas_call | solution.py:477
  24.8 0.8 %pass_on.1 = (f32[16,32,128]{2,1,0:T(8,128)}, f32[32,128]{1,0:T(8,128)}, f32[3,128,128]{2,1,0:T(8,128)}, f32[6,128]{1,0:T(8,128)}) custom-call(f32[16,48,128]{2,1,0:T(8,128)S(1)} %get-tuple-element.8.refs_0_, f32[32,128]{1,0:T(8,128)S(1)} %get-tuple-element.9.refs_1_, f32[3,128,128]{2,1,0:T(8,128)S(1)} %get-tuple-element.10.refs_2_, ...), custom_call_target="tpu_custom_call" | custom-call | tf_op jit(solution)/shard_map/pass_on/pallas_call | solution.py:504
